TPU v7x, 768 devices: a whole 4x8x12 slice. The times are simulated.
768 devices in a mesh: lat: 24 (over z_lo, y), lon: 32 (over z_hi, x, core).
Axes of the slice: x: 4, y: 8, z: 12 (z_hi: 4, z_lo: 3; z = z_hi * 3 + z_lo), core: 2. Of those that a mesh axis runs over, the one named last changes fastest.
Arguments:
- latent_field: bfloat16 [640, 192, 384], P(None, 'lat', 'lon'), may hold values from -6 to 6
- spectral_filter: float32 [640, 192], P('lon'), may hold values from -5 to 5
- conv_weight: float32 [9, 640], replicated, may hold values from -2 to 2
- norm_gain: float32 [640], replicated, may hold values from 0.1 to 1.9
- weight_in: bfloat16 [640, 1280], replicated, may hold values from -0.25 to 0.25
- weight_out: bfloat16 [1280, 640], replicated, may hold values from -0.15625 to 0.15625
Outputs:
- updated: bfloat16 [640, 192, 384], P(None, 'lat', 'lon')
All inputs are finite; a program needn't handle non-finite values.
Results may differ from a plain program's by a relative error of at most 0.01.
Values may be sent and summed in bfloat16 or wider, within the bound.
No kernel may reach another device: no remote copies, remote signals or barrier semaphores. Data moves between devices by JAX's collectives and lax.ppermute only.
A program may use at most 128 MiB of HBM per device.

v0:
```python
import math

import jax
import jax.numpy as jnp
from jax import lax
from jax.sharding import Mesh
from jax.sharding import PartitionSpec as P

LON = ("lon_0", "lon_1", "lon_2")


highest = lax.Precision.HIGHEST
epsilon_norm = 1e-06


def split_up(x, dim, devices):
    shape = x.shape
    pieces = x.reshape(*shape[:dim], devices, shape[dim] // devices, *shape[dim + 1 :])
    return jnp.moveaxis(pieces, dim, 0)


def in_order(pieces, dim):
    pieces = jnp.moveaxis(pieces, 0, dim)
    shape = pieces.shape
    return pieces.reshape(*shape[:dim], shape[dim] * shape[dim + 1], *shape[dim + 2 :])


def exchange_in_order(pieces, axes, turns):
    inside = pieces.shape[1:]
    filled = pieces.reshape(*(lax.axis_size(a) for a in axes), *inside)
    for k in turns:
        filled = lax.all_to_all(filled, axes[k], k, k, tiled=True)
    return filled.reshape(-1, *inside)


def two_step_exchange(x, groups, turns, split_dim, concat_dim):
    devices = lax.axis_size(groups[0]) * lax.axis_size(groups[1])
    pieces = split_up(x, split_dim, devices)
    return in_order(exchange_in_order(pieces, groups, turns), concat_dim)


def with_halo(cells, sides, width):
    for axis, dim in sides:
        count = lax.axis_size(axis)
        ends = count - 1
        head = lax.slice_in_dim(cells, 0, width, axis=dim)
        tail = lax.slice_in_dim(cells, cells.shape[dim] - width, cells.shape[dim], axis=dim)
        cells = jnp.concatenate(
            [
                lax.ppermute(tail, axis, [(i, (i + 1) % count) for i in range(ends)]),
                cells,
                lax.ppermute(head, axis, [((i + 1) % count, i) for i in range(ends)]),
            ],
            axis=dim,
        )
    return cells


def in_one_piece(arrays, axis, split_dim, concat_dim, along):
    widths = [a.shape[along] for a in arrays]
    both = jnp.concatenate(arrays, axis=along)
    filled = lax.all_to_all(both, axis, split_axis=split_dim, concat_axis=concat_dim, tiled=True)
    return tuple(jnp.split(filled, [sum(widths[:k]) for k in range(1, len(widths))], axis=along))


def quadrature(lat_count):
    colatitude = (jnp.arange(lat_count, dtype=jnp.float32) + 0.5) * (math.pi / lat_count)
    return jnp.sin(colatitude) * (math.pi / lat_count)


def fourier_tables(lon_count, mode_count):
    wave_index = (
        jnp.arange(mode_count, dtype=jnp.int32)[:, None]
        * jnp.arange(lon_count, dtype=jnp.int32)[None, :]
    )
    phase_angle = (wave_index % lon_count).astype(jnp.float32) * (2.0 * math.pi / lon_count)
    cosine = jnp.cos(phase_angle)
    sine_table = jnp.sin(phase_angle)
    angle_step = 2.0 * math.pi / lon_count
    forward = jnp.concatenate([angle_step * cosine, -angle_step * sine_table], axis=0)
    weight = jnp.where(jnp.arange(mode_count, dtype=jnp.int32) == 0, 1.0, 2.0).astype(jnp.float32)[
        :, None
    ]
    inverse = jnp.concatenate([weight * cosine, -weight * sine_table], axis=0)
    return (forward, inverse)


def legendre_rows(order_ids, lat_count):
    colatitude = (jnp.arange(lat_count, dtype=jnp.float32) + 0.5) * (math.pi / lat_count)
    cosine = jnp.cos(colatitude)
    sine_col = jnp.sin(colatitude)
    order_f = order_ids.astype(jnp.float32)
    factor_index = jnp.arange(1, lat_count, dtype=jnp.float32)
    ratio_log = jnp.log((2.0 * factor_index - 1.0) / (2.0 * factor_index))
    included = (factor_index[None, :] <= order_f[:, None]).astype(jnp.float32)
    log_factor = jnp.sum(included * ratio_log[None, :], axis=1)
    start_log = 0.5 * jnp.log((2.0 * order_f + 1.0) / (4.0 * math.pi)) + 0.5 * log_factor
    start_log = start_log[:, None] + order_f[:, None] * jnp.log(sine_col)[None, :]
    blank_rows = jnp.zeros((order_ids.shape[0], lat_count), jnp.float32)
    order_col = order_f[:, None]

    def advance(state_carry, degree):
        before, current, scale_log = state_carry
        degree_f = degree.astype(jnp.float32)
        alpha_term = jnp.sqrt(
            (4.0 * degree_f * degree_f - 1.0)
            / jnp.maximum(degree_f * degree_f - order_col * order_col, 1.0)
        )
        beta_term = jnp.sqrt(
            jnp.maximum((degree_f - 1.0) ** 2 - order_col * order_col, 0.0)
            / jnp.maximum(4.0 * (degree_f - 1.0) ** 2 - 1.0, 1.0)
        )
        stepped = alpha_term * (cosine[None, :] * current - beta_term * before)
        at_start = order_ids[:, None] == degree
        past_start = order_ids[:, None] < degree
        fresh_value = jnp.where(at_start, 1.0, jnp.where(past_start, stepped, 0.0))
        fresh_log = jnp.where(at_start, start_log, scale_log)
        entry_value = fresh_value * jnp.exp(fresh_log)
        rescale = jnp.where(
            past_start | at_start, jnp.maximum(jnp.abs(fresh_value), jnp.abs(current)), 1.0
        )
        return (
            (current / rescale, fresh_value / rescale, fresh_log + jnp.log(rescale)),
            entry_value,
        )

    degrees = jnp.arange(lat_count, dtype=jnp.int32)
    unused, legendre = lax.scan(advance, (blank_rows, blank_rows, blank_rows), degrees, unroll=True)
    return legendre


def filter_modes(banded, legendre, filter_block, quad_weights):
    coefficients = jnp.einsum(
        "lmj,pmcj->pmcl", legendre, banded * quad_weights[None, None, None, :], precision=highest
    )
    coefficients = coefficients * filter_block[None, None, :, :]
    return jnp.einsum("lmj,pmcl->pmcj", legendre, coefficients, precision=highest)


def wrap_columns(extended):
    return jnp.concatenate([extended[:, :, -1:], extended, extended[:, :, :1]], axis=2)


def depthwise_core(extended, kernel, lat_rows, lon_cols):
    accumulated = jnp.zeros((extended.shape[0], lat_rows, lon_cols), jnp.float32)
    for row_shift in range(3):
        for col_shift in range(3):
            piece = extended[
                :, row_shift : row_shift + lat_rows, col_shift : col_shift + lon_cols
            ].astype(jnp.float32)
            accumulated = accumulated + kernel[3 * row_shift + col_shift][:, None, None] * piece
    return accumulated.astype(jnp.bfloat16)


def channel_mlp(summed_low, norm_gain, weight_in, weight_out):
    summed = summed_low.astype(jnp.float32)
    scale_inv = lax.rsqrt(jnp.mean(summed * summed, axis=0, keepdims=True) + epsilon_norm)
    normed = (summed * scale_inv * norm_gain[:, None]).astype(jnp.bfloat16)
    hidden = lax.dot_general(
        weight_in, normed, (((0,), (0,)), ((), ())), preferred_element_type=jnp.float32
    )
    hidden = jax.nn.gelu(hidden, approximate=False).astype(jnp.bfloat16)
    result = summed + lax.dot_general(
        weight_out, hidden, (((0,), (0,)), ((), ())), preferred_element_type=jnp.float32
    )
    return result.astype(jnp.bfloat16)


def add_three(first, second, third):
    total = first.astype(jnp.float32) + second.astype(jnp.float32) + third.astype(jnp.float32)
    return total.astype(jnp.bfloat16)


def on_device(latent_field, spectral_filter, conv_weight, norm_gain, weight_in, weight_out):
    channels, lat_rows, lon_cols = latent_field.shape
    sector_count = lax.axis_size(LON)
    lat_count = lat_rows * lax.axis_size("lat")
    lon_count = lon_cols * sector_count
    chan_block = channels // sector_count
    spread = two_step_exchange(latent_field, (("lon_0", "lon_1"), "lon_2"), (0, 1), 0, 2)
    forward, inverse = fourier_tables(lon_count, lat_count)
    flattened = spread.astype(jnp.float32).reshape(chan_block * lat_rows, lon_count)
    spectrum = lax.dot_general(forward, flattened, (((1,), (1,)), ((), ())), precision=highest)
    spectrum = spectrum.reshape(2, lat_count, chan_block, lat_rows)
    banded = lax.all_to_all(spectrum, "lat", split_axis=1, concat_axis=3, tiled=True)
    order_ids = lax.axis_index("lat") * lat_rows + jnp.arange(lat_rows, dtype=jnp.int32)
    legendre = legendre_rows(order_ids, lat_count)
    synthesized = filter_modes(banded, legendre, spectral_filter, quadrature(lat_count))
    regathered = lax.all_to_all(synthesized, "lat", split_axis=3, concat_axis=1, tiled=True)
    regridded = lax.dot_general(
        regathered.reshape(2 * lat_count, chan_block * lat_rows),
        inverse,
        (((0,), (0,)), ((), ())),
        precision=highest,
    )
    spectral = regridded.reshape(chan_block, lat_rows, lon_count).astype(jnp.bfloat16)
    own_kernel = lax.dynamic_slice_in_dim(
        conv_weight, lax.axis_index(LON) * chan_block, chan_block, 1
    )
    rimmed = with_halo(spread, (("lat", 1),), 1)
    sector_mix = depthwise_core(wrap_columns(rimmed), own_kernel, lat_rows, lon_count)
    spectral, local_mix = in_one_piece((spectral, sector_mix), LON, 2, 0, 1)
    summed = add_three(latent_field, spectral, local_mix)
    summed = summed.reshape(channels, lat_rows * lon_cols)
    result = channel_mlp(summed, norm_gain, weight_in, weight_out)
    return result.reshape(channels, lat_rows, lon_cols)


def solution(mesh):
    finer = Mesh(
        mesh.devices.reshape(mesh.shape["lat"], 4, 4, 2), ("lat", "lon_0", "lon_1", "lon_2")
    )
    in_specs = (P(None, "lat", LON), P(LON, None), P(), P(), P(), P())
    out_specs = P(None, "lat", LON)
    return jax.shard_map(
        on_device, mesh=finer, in_specs=in_specs, out_specs=out_specs, check_vma=False
    )
```

profile of v0, /device:TPU:1, one launch (start us, length us, event | category | flops | bytes accessed | tf_op | source)
XLA Modules:
  0.0 597.6 jit_solution(16927545903297105940)
XLA Ops:
  0.0 2.9 reshape_reshape.3
  3.6 2.3 reshape.39293
  5.9 17.8 %all-to-all-start = ((bf16[16,2,1920]{2,1,0:T(2,128)(2,1)}), bf16[16,2,1920]{2,1,0:T(2,128)(2,1)S(1)}, u32[]{:S(2)}, u32[]{:S(2)}) async-start(bf16[16,2,1920]{2,1,0:T(2,128)(2,1)} %reshape.39293), calls=%async_computation | async-start | bytes 245760 | tf_op jit(solution)/shard_map/all_to_all | solution.py:32
  322.1 3.4 multiply_bitcast_fusion.143
  326.7 4.6 multiply_bitcast_fusion.95
  332.9 3.5 multiply_bitcast_fusion.47
  360.6 4.2 exponential_multiply_fusion
  441.3 2.0 reshape.39294
  445.4 4.4 all_to_all.61
  449.8 2.0 reshape.39296
  454.1 2.0 copy.1115
  456.1 3.7 reshape.39297
  459.8 8.6 %all-to-all-start.2 = ((f32[24,1,2560]{2,1,0:T(1,128)}), f32[24,1,2560]{2,1,0:T(1,128)}, u32[]{:S(2)}, u32[]{:S(2)}) async-start(f32[24,1,2560]{2,1,0:T(1,128)} %reshape.39297), calls=%async_computation.2 | async-start | bytes 491520 | tf_op jit(solution)/shard_map/all_to_all | solution.py:185
  468.5 20.0 %concatenate.33 = f32[192,8,192]{2,0,1:T(8,128)S(1)} concatenate(f32[1,8,192]{2,0,1:T(1,128)S(1)} %get-tuple-element.1188, f32[1,8,192]{2,0,1:T(1,128)S(1)} %bitcast.789, f32[1,8,192]{2,0,1:T(1,128)S(1)} %bitcast.790, f32[1,8,192]{2,0,1:T(1,128)S(1)} %bitcast.791, f32[1,8,192]{2,0,1:T(1,128)S(1)} %bitcast.792, f32[1,8,192]{2,0,1:T(1,128)S(1)} %bitcast.793, ...), dimensions={0} | concatenate | bytes 2359296 | tf_op jit(solution)/shard_map/concatenate | solution.py:128
  488.5 2.0 fusion.48
  492.8 2.9 reduce.1
  495.6 4.0 reshape.39298
  499.7 4.1 fusion.13
  505.6 2.7 copy.1289
  508.3 3.4 reshape.39299
  511.7 8.6 %all-to-all-start.3 = ((f32[24,1,2560]{2,1,0:T(1,128)}), f32[24,1,2560]{2,1,0:T(1,128)S(1)}, u32[]{:S(2)}, u32[]{:S(2)}) async-start(f32[24,1,2560]{2,1,0:T(1,128)} %reshape.39299), calls=%async_computation.3 | async-start | bytes 491520 | tf_op jit(solution)/shard_map/all_to_all | solution.py:189
  520.4 3.2 collective-permute-start
  526.7 2.3 collective-permute-done.1
  532.0 2.6 reshape.39300
  536.3 6.0 %copy.1291 = f32[2,24,8,20,8]{2,1,0,4,3:T(8,128)} copy(f32[2,24,8,20,8]{3,4,1,2,0:T(8,128)} %bitcast.766) | data formatting | bytes 491520 | tf_op jit(solution)/shard_map/all_to_all | solution.py:189
  542.3 3.6 reshape.39286
  548.1 3.4 reshape.39301
  551.5 30.7 %all_to_all.62 = bf16[32,2,1920]{2,1,0:T(2,128)(2,1)} all-to-all(bf16[32,2,1920]{2,1,0:T(2,128)(2,1)S(1)} %reshape.39301), channel_id=1, replica_groups=mesh['lat'=24,'lon_0'=4,'lon_1'=4,'lon_2'=2] {'lon_0','lon_1','lon_2'}, dimensions={0} | all-to-all | bytes 491520 | tf_op jit(solution)/shard_map/all_to_all | solution.py:62
  582.2 4.9 reshape.39302
  587.1 2.3 copy.1294
  589.4 3.7 all_to_all.55
  593.5 3.1 fusion.19
  (757 shorter events, 298.3 us)
Async XLA Ops:
  0.0 593.5 %copy-start = (bf16[1280,640]{1,0:T(8,128)(2,1)S(1)}, bf16[1280,640]{1,0:T(8,128)(2,1)}, u32[]{:S(2)}) copy-start(bf16[1280,640]{1,0:T(8,128)(2,1)} %param.11) | copy-start | bytes 4915204
  5.9 435.4 %all-to-all-start = ((bf16[16,2,1920]{2,1,0:T(2,128)(2,1)}), bf16[16,2,1920]{2,1,0:T(2,128)(2,1)S(1)}, u32[]{:S(2)}, u32[]{:S(2)}) async-start(bf16[16,2,1920]{2,1,0:T(2,128)(2,1)} %reshape.39293), calls=%async_computation | async-start | bytes 245760 | tf_op jit(solution)/shard_map/all_to_all | solution.py:32
  336.4 23.8 %copy-start.8 = (pred[8]{0:T(512)(128)(4,1)S(1)}, pred[8]{0:T(512)(128)(4,1)}, u32[]{:S(2)}) copy-start(pred[8]{0:T(512)(128)(4,1)} %get-tuple-element.99) | copy-start | bytes 28
  336.4 23.8 %copy-start.9 = (pred[8]{0:T(512)(128)(4,1)S(1)}, pred[8]{0:T(512)(128)(4,1)}, u32[]{:S(2)}) copy-start(pred[8]{0:T(512)(128)(4,1)} %get-tuple-element.107) | copy-start | bytes 28
  336.4 23.8 %copy-start.10 = (pred[8]{0:T(512)(128)(4,1)S(1)}, pred[8]{0:T(512)(128)(4,1)}, u32[]{:S(2)}) copy-start(pred[8]{0:T(512)(128)(4,1)} %get-tuple-element.1881) | copy-start | bytes 28
  336.4 23.8 %copy-start.11 = (pred[8]{0:T(512)(128)(4,1)S(1)}, pred[8]{0:T(512)(128)(4,1)}, u32[]{:S(2)}) copy-start(pred[8]{0:T(512)(128)(4,1)} %get-tuple-element.1882) | copy-start | bytes 28
  336.4 23.8 %copy-start.12 = (pred[8]{0:T(512)(128)(4,1)S(1)}, pred[8]{0:T(512)(128)(4,1)}, u32[]{:S(2)}) copy-start(pred[8]{0:T(512)(128)(4,1)} %get-tuple-element.1883) | copy-start | bytes 28
  336.4 23.8 %copy-start.13 = (pred[8]{0:T(512)(128)(4,1)S(1)}, pred[8]{0:T(512)(128)(4,1)}, u32[]{:S(2)}) copy-start(pred[8]{0:T(512)(128)(4,1)} %get-tuple-element.111) | copy-start | bytes 28
  336.4 23.8 %copy-start.14 = (pred[8]{0:T(512)(128)(4,1)S(1)}, pred[8]{0:T(512)(128)(4,1)}, u32[]{:S(2)}) copy-start(pred[8]{0:T(512)(128)(4,1)} %get-tuple-element.113) | copy-start | bytes 28
  336.5 23.8 %copy-start.15 = (pred[8]{0:T(512)(128)(4,1)S(1)}, pred[8]{0:T(512)(128)(4,1)}, u32[]{:S(2)}) copy-start(pred[8]{0:T(512)(128)(4,1)} %get-tuple-element.1884) | copy-start | bytes 28
  336.5 23.8 %copy-start.16 = (pred[8]{0:T(512)(128)(4,1)S(1)}, pred[8]{0:T(512)(128)(4,1)}, u32[]{:S(2)}) copy-start(pred[8]{0:T(512)(128)(4,1)} %get-tuple-element.1885) | copy-start | bytes 28
  336.5 23.8 %copy-start.17 = (pred[8]{0:T(512)(128)(4,1)S(1)}, pred[8]{0:T(512)(128)(4,1)}, u32[]{:S(2)}) copy-start(pred[8]{0:T(512)(128)(4,1)} %get-tuple-element.1886) | copy-start | bytes 28
  336.5 23.8 %copy-start.18 = (pred[8]{0:T(512)(128)(4,1)S(1)}, pred[8]{0:T(512)(128)(4,1)}, u32[]{:S(2)}) copy-start(pred[8]{0:T(512)(128)(4,1)} %get-tuple-element.117) | copy-start | bytes 28
  336.5 23.8 %copy-start.19 = (pred[8]{0:T(512)(128)(4,1)S(1)}, pred[8]{0:T(512)(128)(4,1)}, u32[]{:S(2)}) copy-start(pred[8]{0:T(512)(128)(4,1)} %get-tuple-element.119) | copy-start | bytes 28
  336.5 23.8 %copy-start.20 = (pred[8]{0:T(512)(128)(4,1)S(1)}, pred[8]{0:T(512)(128)(4,1)}, u32[]{:S(2)}) copy-start(pred[8]{0:T(512)(128)(4,1)} %get-tuple-element.1887) | copy-start | bytes 28
  336.5 23.8 %copy-start.21 = (pred[8]{0:T(512)(128)(4,1)S(1)}, pred[8]{0:T(512)(128)(4,1)}, u32[]{:S(2)}) copy-start(pred[8]{0:T(512)(128)(4,1)} %get-tuple-element.1888) | copy-start | bytes 28
  336.5 23.8 %copy-start.22 = (pred[8]{0:T(512)(128)(4,1)S(1)}, pred[8]{0:T(512)(128)(4,1)}, u32[]{:S(2)}) copy-start(pred[8]{0:T(512)(128)(4,1)} %get-tuple-element.1889) | copy-start | bytes 28
  336.5 23.8 %copy-start.23 = (pred[8]{0:T(512)(128)(4,1)S(1)}, pred[8]{0:T(512)(128)(4,1)}, u32[]{:S(2)}) copy-start(pred[8]{0:T(512)(128)(4,1)} %get-tuple-element.123) | copy-start | bytes 28
  336.5 23.8 %copy-start.24 = (pred[8]{0:T(512)(128)(4,1)S(1)}, pred[8]{0:T(512)(128)(4,1)}, u32[]{:S(2)}) copy-start(pred[8]{0:T(512)(128)(4,1)} %get-tuple-element.125) | copy-start | bytes 28
  336.6 23.8 %copy-start.25 = (pred[8]{0:T(512)(128)(4,1)S(1)}, pred[8]{0:T(512)(128)(4,1)}, u32[]{:S(2)}) copy-start(pred[8]{0:T(512)(128)(4,1)} %get-tuple-element.1890) | copy-start | bytes 28
  336.6 23.8 %copy-start.26 = (pred[8]{0:T(512)(128)(4,1)S(1)}, pred[8]{0:T(512)(128)(4,1)}, u32[]{:S(2)}) copy-start(pred[8]{0:T(512)(128)(4,1)} %get-tuple-element.1891) | copy-start | bytes 28
  336.6 23.8 %copy-start.27 = (pred[8]{0:T(512)(128)(4,1)S(1)}, pred[8]{0:T(512)(128)(4,1)}, u32[]{:S(2)}) copy-start(pred[8]{0:T(512)(128)(4,1)} %get-tuple-element.1892) | copy-start | bytes 28
  336.6 23.8 %copy-start.28 = (pred[8]{0:T(512)(128)(4,1)S(1)}, pred[8]{0:T(512)(128)(4,1)}, u32[]{:S(2)}) copy-start(pred[8]{0:T(512)(128)(4,1)} %get-tuple-element.129) | copy-start | bytes 28
  336.6 23.8 %copy-start.29 = (pred[8]{0:T(512)(128)(4,1)S(1)}, pred[8]{0:T(512)(128)(4,1)}, u32[]{:S(2)}) copy-start(pred[8]{0:T(512)(128)(4,1)} %get-tuple-element.131) | copy-start | bytes 28
  336.6 23.8 %copy-start.30 = (pred[8]{0:T(512)(128)(4,1)S(1)}, pred[8]{0:T(512)(128)(4,1)}, u32[]{:S(2)}) copy-start(pred[8]{0:T(512)(128)(4,1)} %get-tuple-element.1893) | copy-start | bytes 28
  336.6 23.8 %copy-start.31 = (pred[8]{0:T(512)(128)(4,1)S(1)}, pred[8]{0:T(512)(128)(4,1)}, u32[]{:S(2)}) copy-start(pred[8]{0:T(512)(128)(4,1)} %get-tuple-element.1894) | copy-start | bytes 28
  336.6 23.8 %copy-start.32 = (pred[8]{0:T(512)(128)(4,1)S(1)}, pred[8]{0:T(512)(128)(4,1)}, u32[]{:S(2)}) copy-start(pred[8]{0:T(512)(128)(4,1)} %get-tuple-element.1895) | copy-start | bytes 28
  336.6 23.8 %copy-start.33 = (pred[8]{0:T(512)(128)(4,1)S(1)}, pred[8]{0:T(512)(128)(4,1)}, u32[]{:S(2)}) copy-start(pred[8]{0:T(512)(128)(4,1)} %get-tuple-element.135) | copy-start | bytes 28
  459.8 32.4 %all-to-all-start.2 = ((f32[24,1,2560]{2,1,0:T(1,128)}), f32[24,1,2560]{2,1,0:T(1,128)}, u32[]{:S(2)}, u32[]{:S(2)}) async-start(f32[24,1,2560]{2,1,0:T(1,128)} %reshape.39297), calls=%async_computation.2 | async-start | bytes 491520 | tf_op jit(solution)/shard_map/all_to_all | solution.py:185
  511.7 19.2 %all-to-all-start.3 = ((f32[24,1,2560]{2,1,0:T(1,128)}), f32[24,1,2560]{2,1,0:T(1,128)S(1)}, u32[]{:S(2)}, u32[]{:S(2)}) async-start(f32[24,1,2560]{2,1,0:T(1,128)} %reshape.39299), calls=%async_computation.3 | async-start | bytes 491520 | tf_op jit(solution)/shard_map/all_to_all | solution.py:189
  520.4 6.3 %collective-permute-start = (bf16[20,1,384]{2,1,0:T(2,128)(2,1)S(1)}, bf16[20,1,384]{2,1,0:T(2,128)(2,1)S(1)}, u32[]{:S(2)}, u32[]{:S(2)}) collective-permute-start(bf16[20,1,384]{2,1,0:T(2,128)(2,1)S(1)} %get-tuple-element.1012), channel_id=1, source_target_pairs={{0,32},{32,64},{64,96},{96,128},{128,160},{160,192},{192,224},{224... | collective-permute-start | bytes 46088 | tf_op jit(solution)/shard_map/ppermute | solution.py:50
  523.6 5.5 collective-permute-start.1
  (60 other events, 775.8 us)
where the time goes:
time: 609 us; the launch traced here: 598 us
  other arithmetic  202 us (33%)
  local copies, waits for them, and re-layouts  182 us (30%)
  between operations  125 us (21%)
  starting transfers between devices  39.7 us (7%)
  blocking collectives  35.2 us (6%)
  matrix products  11.3 us (2%)
    or x96, other arithmetic, advance(): past_start | at_start  164 us
    broadcast_in_dim x171, local copies, waits for them, and re-layouts, legendre_rows(): lax.scan(advance, (blank_rows, blank_rows, blank_rows), degrees, unroll=T...  91.2 us
    all_to_all x1, blocking collectives, in_one_piece(): lax.all_to_all(both, axis, split_axis=split_dim, concat_axis=concat_dim,...  30.7 us
    unnamed x184, local copies, waits for them, and re-layouts  30.2 us
    concatenate x1, local copies, waits for them, and re-layouts, legendre_rows(): lax.scan(advance, (blank_rows, blank_rows, blank_rows), degrees, unroll=T...  20 us
    all_to_all x1, starting transfers between devices, exchange_in_order(): filled = lax.all_to_all(filled, axes[k], k, k, tiled=True)  17.8 us
    broadcast_in_dim x32, other arithmetic, legendre_rows(): lax.scan(advance, (blank_rows, blank_rows, blank_rows), degrees, unroll=T...  13.8 us
  transfers between devices with their start and end apart: 5, of which 2 were waited for; matrix products, arithmetic and copies ran while one was open for 54% of the time, Pallas kernels for 0%

commit v1 on v0

v1 whole, which is shorter than its diff:
```python
import functools
import math

import jax
import jax.numpy as jnp
from jax import lax
from jax.experimental import pallas as pl
from jax.experimental.pallas import tpu as pltpu
from jax.sharding import PartitionSpec as P

LON, LAT, COLS, ROWS, CHAN = 32, 24, 12, 8, 20
NLON, NLAT = LON * COLS, LAT * ROWS
PAIRS = COLS // 2
BF, F32 = jnp.bfloat16, jnp.float32
EPS = 1e-06


def lanes_of(shape):
    return lax.broadcasted_iota(jnp.int32, shape, 1)


def inside(shape, start, width):
    lane = lanes_of(shape)
    return (lane >= start) & (lane < start + width)


def turn(x, shift):
    shift %= 128
    return x if shift == 0 else pltpu.roll(x, shift, 1)


def call(body, outs, *args, scratch=(), name, mib=24, flops=0, in_specs=None):
    if in_specs is None:
        in_specs = [pl.BlockSpec(memory_space=pltpu.VMEM)] * len(args)
    single = isinstance(outs, tuple)
    result = pl.pallas_call(
        body,
        out_shape=[jax.ShapeDtypeStruct(*o) for o in ([outs] if single else outs)],
        in_specs=in_specs,
        out_specs=[pl.BlockSpec(memory_space=pltpu.VMEM)] * (1 if single else len(outs)),
        scratch_shapes=list(scratch),
        compiler_params=pltpu.CompilerParams(vmem_limit_bytes=mib * 2**20),
        cost_estimate=pl.CostEstimate(flops=flops, bytes_accessed=1_000_000, transcendentals=0),
        name=name,
    )(*args)
    return result[0] if single else result


def pack_body(x_ref, send_ref):
    shape = (16, 128)
    for d in range(LON):
        tile, off = divmod(CHAN * d, 128)
        total = jnp.zeros(shape, F32)
        for q in range(PAIRS):
            at = slice(16 * q, 16 * q + 16)
            piece = x_ref[at, 128 * tile : 128 * tile + 128].astype(F32)
            if off + CHAN > 128:
                after = x_ref[at, 128 * tile + 128 : 128 * tile + 256].astype(F32)
                piece = jnp.where(lanes_of(shape) >= off, piece, after)
            total = jnp.where(inside(shape, CHAN * q, CHAN), turn(piece, CHAN * q - off), total)
        send_ref[d] = total.astype(BF)


def wave(order, part, column):
    v = (order * column + part * (NLON // 4)).astype(F32)
    index = v - NLON * jnp.floor(v * (1.0 / NLON))
    x = (NLON // 4 - jnp.abs(index - NLON // 2)) * (2.0 * math.pi / NLON)
    y = x * x
    s = 1.0 / 6227020800.0
    for term in (-1.0 / 39916800.0, 1.0 / 362880.0, -1.0 / 5040.0, 1.0 / 120.0, -1.0 / 6.0, 1.0):
        s = s * y + term
    return -(s * x)


def mode_of(n):
    return ((n >> 4) << 3) + (n & 7), (n >> 3) & 1


def column_of(k):
    return COLS * (k & 31) + (k >> 5)


def halves(x):
    high = x.astype(BF)
    return high, (x - high.astype(F32)).astype(BF)


def fourier_body(fhi_ref, flo_ref, ihi_ref, ilo_ref):
    shape = (16, NLON)
    lane = lanes_of(shape)

    def block(b, unused):
        row = lax.broadcasted_iota(jnp.int32, shape, 0) + 16 * b
        at = pl.ds(pl.multiple_of(16 * b, 16), 16)
        order, part = mode_of(row)
        table = wave(order, part, column_of(lane)) * (2.0 * math.pi / NLON)
        fhi_ref[at, :], flo_ref[at, :] = halves(table)
        order, part = mode_of(lane)
        table = wave(order, part, column_of(row)) * jnp.where(order == 0, 1.0, 2.0)
        ihi_ref[at, :], ilo_ref[at, :] = halves(table)
        return unused

    lax.fori_loop(0, NLON // 16, block, 0)


def legendre_body(band_ref, pw_ref, pt_ref, table):
    shape = (8, 256)
    lane = lanes_of(shape)
    order_i = lax.broadcasted_iota(jnp.int32, shape, 0) + band_ref[0] * 8
    order = order_i.astype(F32)
    r = jnp.floor((lane.astype(F32) + 0.5) * (1.0 / LAT))
    row = jnp.minimum(8.0 * (lane.astype(F32) - LAT * r) + r, NLAT - 1.0)
    theta = (row + 0.5) * (math.pi / NLAT)
    cosine, sine = jnp.cos(theta), jnp.sin(theta)
    k = lane.astype(F32) + 1.0
    ratio = jnp.log((2.0 * k - 1.0) / (2.0 * k))
    factor = jnp.sum(jnp.where(k <= order, ratio, 0.0), axis=1, keepdims=True)
    start = 0.5 * jnp.log((2.0 * order + 1.0) / (4.0 * math.pi)) + 0.5 * factor + order * jnp.log(sine)
    square = order * order
    every = 16

    def block(b, carry):
        before, current, log_scale = carry
        scale = jnp.exp(log_scale)
        for t in range(every):
            degree = b * every + t
            l = degree.astype(F32)
            lower = (l - 1.0) * (l - 1.0)
            alpha = jnp.sqrt((4.0 * l * l - 1.0) / jnp.maximum(l * l - square, 1.0))
            beta = jnp.sqrt(jnp.maximum(lower - square, 0.0) / jnp.maximum(4.0 * lower - 1.0, 1.0))
            fresh = (alpha * cosine) * current - (alpha * beta) * before
            fresh = jnp.where(order_i == degree, 1.0, fresh)
            fresh = jnp.where(order_i > degree, 0.0, fresh)
            before, current = current, fresh
            entry = fresh * scale
            for h in range(2):
                table[pl.ds(pl.multiple_of(2048 * h + degree * 8, 8), 8), :] = entry[:, 128 * h : 128 * h + 128]
        largest = jnp.maximum(jnp.abs(before), jnp.abs(current))
        largest = jnp.where(order_i <= b * every + (every - 1), largest, 1.0)
        return before / largest, current / largest, log_scale + jnp.log(largest)

    blank = jnp.zeros(shape, F32)
    lax.fori_loop(0, NLAT // every, block, (blank, blank, start))
    for h in range(2):
        table[2048 * h + NLAT * 8 : 2048 * h + 2048, :] = jnp.zeros((64 * 8, 128), F32)
    weight = jnp.where(lane < NLAT, sine * (math.pi / NLAT), 0.0)[0:1, :]
    for m in range(8):
        p = jnp.concatenate([table[pl.ds(2048 * h + m, 256, stride=8), :] for h in range(2)], axis=1)
        pw_ref[m] = (p * weight).astype(BF)
        pt_ref[m] = jnp.transpose(p)[:NLAT, :].astype(BF)


def spectrum_body(recv_ref, fhi_ref, flo_ref, full_ref, send_ref, first_ref, last_ref, wide):
    wide[...] = recv_ref[...].astype(F32).reshape(LON * 16, 128)
    shape = (LON, 128)
    for e in range(2):
        for h in range(2):
            total = [jnp.zeros(shape, F32)] * PAIRS
            for s in range(4):
                rows = wide[pl.ds(8 * e + 4 * h + s, LON, stride=16), :]
                for q in range(PAIRS):
                    total[q] = jnp.where(inside(shape, 32 * s, CHAN), turn(rows, 32 * s - CHAN * q), total[q])
            for q in range(PAIRS):
                kap = 2 * q + e
                full_ref[32 * kap : 32 * kap + 32, 128 * h : 128 * h + 128] = total[q].astype(BF)
    full = full_ref[...]
    spectrum = jnp.dot(fhi_ref[...], full, preferred_element_type=F32)
    spectrum = spectrum + jnp.dot(flo_ref[...], full, preferred_element_type=F32)
    send_ref[...] = spectrum.astype(BF).reshape(LAT, 16, 256)
    shape = (96, 128)
    for edge_ref, at, own in ((first_ref, 0, 0), (last_ref, 128, 96)):
        edge = jnp.zeros(shape, F32)
        for g in range(4):
            rows = full_ref[96 * g : 96 * g + 96, at : at + 128].astype(F32)
            edge = jnp.where(inside(shape, 32 * g, 32), turn(rows, 32 * g - own), edge)
        edge_ref[...] = edge.astype(BF)


def filter_body(recv_ref, pw_ref, pt_ref, gain_ref, send_ref, wide, out):
    rows = LAT * 16
    for h in range(2):
        wide[rows * h : rows * h + rows, :] = recv_ref[:, :, 128 * h : 128 * h + 128].astype(F32).reshape(rows, 128)
    gain = gain_ref[...]
    shape = (LAT, 128)
    lane = lanes_of(shape)
    for m in range(8):
        chunks = []
        for h in range(2):
            low, high = (wide[pl.ds(rows * h + 8 * p + m, LAT, stride=16), :] for p in range(2))
            for s in range(4):
                chunks.append(jnp.where(lane < 32, turn(low, -32 * s), turn(high, 32 - 32 * s)))
        chunks.append(jnp.zeros((256 - NLAT, 128), F32))
        field = jnp.concatenate(chunks, axis=0).astype(BF)
        coefficients = jnp.dot(pw_ref[m], field, preferred_element_type=F32) * gain
        back = jnp.dot(pt_ref[m], coefficients.astype(BF), preferred_element_type=F32)
        for p in range(2):
            for h in range(2):
                total = jnp.zeros(shape, F32)
                for s in range(4):
                    r = 4 * h + s
                    total = jnp.where(
                        inside(shape, 32 * s, 32), turn(back[LAT * r : LAT * r + LAT, :], 32 * s - 32 * p), total
                    )
                out[pl.ds(rows * h + 8 * p + m, LAT, stride=16), :] = total
    for h in range(2):
        send_ref[:, :, 128 * h : 128 * h + 128] = out[rows * h : rows * h + rows, :].astype(BF).reshape(LAT, 16, 128)


def local_body(full_ref, above_ref, below_ref, taps_ref, base_ref, up, down):
    shape = (96, 128)
    lane = lanes_of(shape)
    for g in range(4):
        at = slice(96 * g, 96 * g + 96)
        left, right = full_ref[at, 0:128].astype(F32), full_ref[at, 128:256].astype(F32)
        above, below = above_ref[...].astype(F32), below_ref[...].astype(F32)
        up[at, 0:128] = jnp.where(lane < 32, turn(above, -32 * g), turn(left, 32))
        up[at, 128:256] = jnp.where(lane < 32, turn(left, 32), turn(right, 32))
        down[at, 0:128] = jnp.where(lane >= 96, turn(right, 96), turn(left, 96))
        down[at, 128:256] = jnp.where(lane >= 96, turn(below, 96 - 32 * g), turn(right, 96))

    def mixed(kap, b):
        at = slice(32 * kap, 32 * kap + 32)
        rows = (up[at, :], full_ref[at, :].astype(F32), down[at, :])
        return sum(taps_ref[3 * i + b : 3 * i + b + 1, :] * rows[i] for i in range(3))

    for kap in range(COLS):
        west = mixed(kap - 1, 0) if kap > 0 else pltpu.roll(mixed(COLS - 1, 0), 1, 0)
        east = mixed(kap + 1, 2) if kap < COLS - 1 else pltpu.roll(mixed(0, 2), LON - 1, 0)
        at = slice(32 * kap, 32 * kap + 32)
        base_ref[at, :] = full_ref[at, :].astype(F32) + (west + mixed(kap, 1) + east)


def synthesis_body(recv_ref, ihi_ref, ilo_ref, base_ref, send_ref, out):
    modes = recv_ref[...].reshape(NLON, 256)
    summed = jnp.dot(ihi_ref[...], modes, preferred_element_type=F32)
    summed = base_ref[...] + (summed + jnp.dot(ilo_ref[...], modes, preferred_element_type=F32))
    shape = (LON, 128)
    for e in range(2):
        for h in range(2):
            for s in range(4):
                total = jnp.zeros(shape, F32)
                for q in range(PAIRS):
                    kap = 2 * q + e
                    rows = summed[32 * kap : 32 * kap + 32, 128 * h : 128 * h + 128]
                    total = jnp.where(inside(shape, CHAN * q, CHAN), turn(rows, CHAN * q - 32 * s), total)
                out[pl.ds(8 * e + 4 * h + s, LON, stride=16), :] = total
    send_ref[...] = out[...].astype(BF).reshape(LON, 16, 128)


def mlp_body(recv_ref, gain_ref, win_ref, wout_ref, out_ref, summed_ref):
    shape = (16, 128)
    lane = lanes_of(shape)
    for tile in range(5):
        for q in range(PAIRS):
            total = jnp.zeros(shape, F32)
            for d in range(128 * tile // CHAN, (128 * tile + 127) // CHAN + 1):
                off = CHAN * d - 128 * tile
                piece = turn(recv_ref[d].astype(F32), off - CHAN * q)
                total = jnp.where((lane >= off) & (lane < off + CHAN), piece, total)
            summed_ref[16 * q : 16 * q + 16, 128 * tile : 128 * tile + 128] = total
    summed = summed_ref[...]
    mean = jnp.sum(summed * summed, axis=1, keepdims=True) * (1.0 / summed.shape[1])
    normed = (summed * lax.rsqrt(mean + EPS) * gain_ref[...]).astype(BF)
    hidden = jnp.dot(normed, win_ref[...], preferred_element_type=F32)
    hidden = (0.5 * hidden * (1.0 + lax.erf(hidden * math.sqrt(0.5)))).astype(BF)
    result = summed + jnp.dot(hidden, wout_ref[...], preferred_element_type=F32)
    out_ref[...] = result.astype(BF)


def on_device(latent_field, spectral_filter, conv_weight, norm_gain, weight_in, weight_out):
    channels = latent_field.shape[0]
    field = jnp.transpose(latent_field, (2, 1, 0)).reshape(COLS * ROWS, channels)
    pieces = call(pack_body, ((LON, 16, 128), BF), field, name="pack")
    pieces = lax.all_to_all(pieces, "lon", 0, 0, tiled=True)

    fhi, flo, ihi, ilo = call(fourier_body, [((NLON, NLON), BF)] * 4, name="fourier_tables", flops=10_000_000)
    band = lax.axis_index("lat").astype(jnp.int32).reshape(1)
    pw, pt = call(
        legendre_body,
        [((8, 256, 256), BF), ((8, NLAT, 256), BF)],
        band,
        scratch=[pltpu.VMEM((2 * 2048, 128), F32)],
        in_specs=[pl.BlockSpec(memory_space=pltpu.SMEM)],
        name="legendre_tables",
        flops=10_000_000,
    )
    gain = jnp.pad(jnp.transpose(spectral_filter), ((0, 64), (0, 32 - CHAN)))
    gain = jnp.tile(gain, (1, 4))
    taps = lax.dynamic_slice_in_dim(conv_weight, lax.axis_index("lon") * CHAN, CHAN, 1)
    taps = jnp.tile(jnp.pad(taps, ((0, 7), (0, 32 - CHAN))), (1, 8))

    full, modes, first, last = call(
        spectrum_body,
        [((NLON, 256), BF), ((LAT, 16, 256), BF), ((96, 128), BF), ((96, 128), BF)],
        pieces,
        fhi,
        flo,
        scratch=[pltpu.VMEM((LON * 16, 128), F32)],
        name="spectrum",
    )
    modes = lax.all_to_all(modes, "lat", 0, 0, tiled=True)
    below = lax.ppermute(first, "lat", [(i + 1, i) for i in range(LAT - 1)])
    above = lax.ppermute(last, "lat", [(i, i + 1) for i in range(LAT - 1)])
    modes = call(
        filter_body,
        ((LAT, 16, 256), BF),
        modes,
        pw,
        pt,
        gain,
        scratch=[pltpu.VMEM((2 * LAT * 16, 128), F32)] * 2,
        name="filter",
    )
    modes = lax.all_to_all(modes, "lat", 0, 0, tiled=True)
    base = call(
        local_body,
        ((NLON, 256), F32),
        full,
        above,
        below,
        taps,
        scratch=[pltpu.VMEM((NLON, 256), F32)] * 2,
        name="local_mix",
        flops=5_000_000,
    )
    pieces = call(
        synthesis_body,
        ((LON, 16, 128), BF),
        modes,
        ihi,
        ilo,
        base,
        scratch=[pltpu.VMEM((LON * 16, 128), F32)],
        name="synthesis",
    )
    pieces = lax.all_to_all(pieces, "lon", 0, 0, tiled=True)
    result = call(
        mlp_body,
        ((COLS * ROWS, channels), BF),
        pieces,
        norm_gain.reshape(1, channels),
        weight_in,
        weight_out,
        scratch=[pltpu.VMEM((COLS * ROWS, channels), F32)],
        name="mlp",
    )
    return jnp.transpose(result.reshape(COLS, ROWS, channels), (2, 1, 0))


def solution(mesh):
    in_specs = (P(None, "lat", "lon"), P("lon", None), P(), P(), P(), P())
    return jax.shard_map(on_device, mesh=mesh, in_specs=in_specs, out_specs=P(None, "lat", "lon"), check_vma=False)
```

time: 609 us -> 104 us (0.17)
  the two profiles are of different devices: /device:TPU:1 before, /device:TPU:25 now
where the time goes in v1:
time: 104 us
  starting transfers between devices  48.8 us (47%)
  waiting for transfers between devices  28.3 us (27%)
  local copies, waits for them, and re-layouts  14.6 us (14%)
  Pallas kernels  11.7 us (11%)
    all_to_all x2, starting transfers between devices, on_device(): pieces = lax.all_to_all(pieces, 'lon', 0, 0, tiled=True)  25.3 us
    all_to_all x2, waiting for transfers between devices, on_device(): pieces = lax.all_to_all(pieces, 'lon', 0, 0, tiled=True)  21.7 us
    all_to_all x2, starting transfers between devices, on_device(): modes = lax.all_to_all(modes, 'lat', 0, 0, tiled=True)  17.2 us
    unnamed x38, local copies, waits for them, and re-layouts  12.2 us
    pallas_call x8, Pallas kernels, call(): pl.pallas_call(body, out_shape=[jax.ShapeDtypeStruct(*o) for o in ([outs]...  11.7 us
    ppermute x1, starting transfers between devices, on_device(): above = lax.ppermute(last, 'lat', [(i, i + 1) for i in range(LAT - 1)])  4.3 us
    all_to_all x2, waiting for transfers between devices, on_device(): modes = lax.all_to_all(modes, 'lat', 0, 0, tiled=True)  4.16 us
    ppermute x1, waiting for transfers between devices, on_device(): below = lax.ppermute(first, 'lat', [(i + 1, i) for i in range(LAT - 1)])  2.5 us
  transfers between devices with their start and end apart: 6, of which 4 were waited for; matrix products, arithmetic and copies ran while one was open for 2% of the time, Pallas kernels for 5%

profile of v1, /device:TPU:25, one launch (start us, length us, event | category | flops | bytes accessed | tf_op | source)
XLA Modules:
  0.0 103.7 jit_solution(9820975767734531929)
XLA Ops:
  0.0 0.9 copy-done.15
  0.9 0.9 pack.1
  1.8 17.8 %all-to-all-start = ((bf16[32,16,128]{2,1,0:T(8,128)(2,1)}), bf16[32,16,128]{2,1,0:T(8,128)(2,1)S(1)}, u32[]{:S(2)}, u32[]{:S(2)}) async-start(bf16[32,16,128]{2,1,0:T(8,128)(2,1)} %pack.1), calls=%async_computation | async-start | bytes 262144 | tf_op jit(solution)/shard_map/all_to_all | solution.py:274
  19.6 1.8 %fourier_tables.1 = (bf16[384,384]{1,0:T(8,128)(2,1)S(1)}, bf16[384,384]{1,0:T(8,128)(2,1)S(1)}, bf16[384,384]{1,0:T(8,128)(2,1)S(1)}, bf16[384,384]{1,0:T(8,128)(2,1)S(1)}) custom-call(), custom_call_target="tpu_custom_call" | custom-call | flops 10000000 | bytes 1000000 | tf_op jit(solution)/shard_map/fourier_tables/pallas_call | solution.py:36
  21.5 0.7 copy-done.9
  22.2 0.7 copy-done.11
  22.9 9.5 %all-to-all-done.recv_ref = bf16[32,16,128]{2,1,0:T(8,128)(2,1)S(1)} async-done(((bf16[32,16,128]{2,1,0:T(8,128)(2,1)}), bf16[32,16,128]{2,1,0:T(8,128)(2,1)S(1)}, u32[]{:S(2)}, u32[]{:S(2)}) %all-to-all-start) | async-done | bytes 131104 | tf_op jit(solution)/shard_map/all_to_all | solution.py:274
  32.5 1.3 %spectrum.1 = (bf16[384,256]{1,0:T(8,128)(2,1)S(1)}, bf16[24,16,256]{2,1,0:T(8,128)(2,1)}, bf16[96,128]{1,0:T(8,128)(2,1)S(1)}, bf16[96,128]{1,0:T(8,128)(2,1)S(1)}) custom-call(bf16[32,16,128]{2,1,0:T(8,128)(2,1)S(1)} %all-to-all-done.recv_ref, bf16[384,384]{1,0:T(8,128)(2,1)S(1)} %get-tuple-element.15.fhi_ref, bf16[384,384]{1,0:T(8,128)(2,1)S(1)} %get-tuple-element.16.flo_ref), custom_call_target="tpu_custom_call" | custom-call | bytes 1000000 | tf_op jit(solution)/shard_map/spectrum/pallas_call | solution.py:36
  33.8 0.7 copy-done.13
  35.7 10.0 %all-to-all-start.1 = ((bf16[24,16,256]{2,1,0:T(8,128)(2,1)}), bf16[24,16,256]{2,1,0:T(8,128)(2,1)S(1)}, u32[]{:S(2)}, u32[]{:S(2)}) async-start(bf16[24,16,256]{2,1,0:T(8,128)(2,1)} %get-tuple-element.17), calls=%async_computation.1 | async-start | bytes 393216 | tf_op jit(solution)/shard_map/all_to_all | solution.py:301
  45.8 2.0 %legendre_tables.1 = (bf16[8,256,256]{2,1,0:T(8,128)(2,1)S(1)}, bf16[8,192,256]{2,1,0:T(8,128)(2,1)S(1)}) custom-call(s32[1]{0:T(128)} %bitcast.2.band_ref), custom_call_target="tpu_custom_call" | custom-call | flops 10000000 | bytes 1000000 | tf_op jit(solution)/shard_map/legendre_tables/pallas_call | solution.py:36
  47.8 0.9 copy-done.6
  48.7 4.2 %all-to-all-done.1.recv_ref = bf16[24,16,256]{2,1,0:T(8,128)(2,1)S(1)} async-done(((bf16[24,16,256]{2,1,0:T(8,128)(2,1)}), bf16[24,16,256]{2,1,0:T(8,128)(2,1)S(1)}, u32[]{:S(2)}, u32[]{:S(2)}) %all-to-all-start.1) | async-done | bytes 196640 | tf_op jit(solution)/shard_map/all_to_all | solution.py:301
  52.8 1.1 %copy-done.7 = bf16[8,192,256]{2,1,0:T(8,128)(2,1)S(1)} copy-done((bf16[8,192,256]{2,1,0:T(8,128)(2,1)S(1)}, bf16[8,192,256]{2,1,0:T(8,128)(2,1)}, u32[]{:S(2)}) %copy-start.7) | copy-done | bytes 786456
  54.0 2.1 %filter.1 = bf16[24,16,256]{2,1,0:T(8,128)(2,1)S(1)} custom-call(bf16[24,16,256]{2,1,0:T(8,128)(2,1)S(1)} %all-to-all-done.1.recv_ref, bf16[8,256,256]{2,1,0:T(8,128)(2,1)S(1)} %get-tuple-element.18.pw_ref, bf16[8,192,256]{2,1,0:T(8,128)(2,1)S(1)} %copy-done.7, f32[256,128]{1,0:T(8,128)S(1)} %copy.8.gain_ref), custom_call_target="tpu_custom_call" | custom-call | bytes 1000000 | tf_op jit(solution)/shard_map/filter/pallas_call | solution.py:36
  56.1 0.7 copy-done.5
  56.7 7.3 %all-to-all-start.2 = ((bf16[24,16,256]{2,1,0:T(8,128)(2,1)}), bf16[24,16,256]{2,1,0:T(8,128)(2,1)S(1)}, u32[]{:S(2)}, u32[]{:S(2)}) async-start(bf16[24,16,256]{2,1,0:T(8,128)(2,1)} %copy-done.5), calls=%async_computation.2 | async-start | bytes 393216 | tf_op jit(solution)/shard_map/all_to_all | solution.py:314
  64.0 4.3 %collective-permute-start = (bf16[96,128]{1,0:T(8,128)(2,1)}, bf16[96,128]{1,0:T(8,128)(2,1)S(1)}, u32[]{:S(2)}, u32[]{:S(2)}) collective-permute-start(bf16[96,128]{1,0:T(8,128)(2,1)} %copy-done.17), channel_id=1, source_target_pairs={{0,32},{32,64},{64,96},{96,128},{128,160},{160,192},{192,224},{224... | collective-permute-start | bytes 73736 | tf_op jit(solution)/shard_map/ppermute | solution.py:303
  68.3 1.9 %collective-permute-start.1 = (bf16[96,128]{1,0:T(8,128)(2,1)}, bf16[96,128]{1,0:T(8,128)(2,1)}, u32[]{:S(2)}, u32[]{:S(2)}) collective-permute-start(bf16[96,128]{1,0:T(8,128)(2,1)} %copy-done.16), channel_id=1, source_target_pairs={{32,0},{64,32},{96,64},{128,96},{160,128},{192,160},{224,192},{256... | collective-permute-start | bytes 73736 | tf_op jit(solution)/shard_map/ppermute | solution.py:302
  71.0 0.9 tile.21.taps_ref
  71.9 2.5 %collective-permute-done.1.below_ref = bf16[96,128]{1,0:T(8,128)(2,1)} collective-permute-done((bf16[96,128]{1,0:T(8,128)(2,1)}, bf16[96,128]{1,0:T(8,128)(2,1)}, u32[]{:S(2)}, u32[]{:S(2)}) %collective-permute-start.1) | collective-permute-done | bytes 24608 | tf_op jit(solution)/shard_map/ppermute | solution.py:302
  74.4 0.9 copy-done.14
  75.3 1.1 %local_mix.1.base_ref = f32[384,256]{1,0:T(8,128)S(1)} custom-call(bf16[384,256]{1,0:T(8,128)(2,1)S(1)} %copy-done.14, bf16[96,128]{1,0:T(8,128)(2,1)S(1)} %collective-permute-done.above_ref, bf16[96,128]{1,0:T(8,128)(2,1)} %collective-permute-done.1.below_ref, f32[16,256]{1,0:T(8,128)S(1)} %tile.21.taps_ref), custom_call_target="tpu_custom_call" | custom-call | flops 5000000 | bytes 1000000 | tf_op jit(solution)/shard_map/local_mix/pallas_call | solution.py:36
  76.5 0.7 copy-done.3
  77.2 1.0 copy-done.4
  78.2 1.0 copy-done.10
  79.2 1.0 copy-done.12
  80.2 0.8 synthesis.1
  81.6 7.5 %all-to-all-start.3 = ((bf16[32,16,128]{2,1,0:T(8,128)(2,1)}), bf16[32,16,128]{2,1,0:T(8,128)(2,1)S(1)}, u32[]{:S(2)}, u32[]{:S(2)}) async-start(bf16[32,16,128]{2,1,0:T(8,128)(2,1)} %copy-done.8), calls=%async_computation.3 | async-start | bytes 262144 | tf_op jit(solution)/shard_map/all_to_all | solution.py:336
  89.1 0.7 reshape.22.gain_ref
  89.8 12.1 %all-to-all-done.3.recv_ref = bf16[32,16,128]{2,1,0:T(8,128)(2,1)S(1)} async-done(((bf16[32,16,128]{2,1,0:T(8,128)(2,1)}), bf16[32,16,128]{2,1,0:T(8,128)(2,1)S(1)}, u32[]{:S(2)}, u32[]{:S(2)}) %all-to-all-start.3) | async-done | bytes 131104 | tf_op jit(solution)/shard_map/all_to_all | solution.py:336
  102.0 1.7 %mlp.1 = bf16[96,640]{1,0:T(8,128)(2,1)} custom-call(bf16[32,16,128]{2,1,0:T(8,128)(2,1)S(1)} %all-to-all-done.3.recv_ref, f32[1,640]{1,0:T(1,128)S(1)} %reshape.22.gain_ref, bf16[640,1280]{1,0:T(8,128)(2,1)S(1)} %copy-done.1, bf16[1280,640]{1,0:T(8,128)(2,1)S(1)} %copy-done.2), custom_call_target="tpu_custom_call" | custom-call | bytes 1000000 | tf_op jit(solution)/shard_map/mlp/pallas_call | solution.py:36
  (34 shorter events, 2.7 us)
Async XLA Ops:
  0.0 70.2 %copy-start = (f32[9,640]{1,0:T(8,128)S(1)}, f32[9,640]{1,0:T(8,128)}, u32[]{:S(2)}) copy-start(f32[9,640]{1,0:T(8,128)} %param.8) | copy-start | bytes 69124
  0.0 0.9 copy-start.15
  0.9 44.7 %copy-start.18 = (f32[20,192]{1,0:T(8,128)S(1)}, f32[20,192]{1,0:T(8,128)}, u32[]{:S(2)}) copy-start(f32[20,192]{1,0:T(8,128)} %param.7) | copy-start | bytes 46084
  1.8 30.6 %all-to-all-start = ((bf16[32,16,128]{2,1,0:T(8,128)(2,1)}), bf16[32,16,128]{2,1,0:T(8,128)(2,1)S(1)}, u32[]{:S(2)}, u32[]{:S(2)}) async-start(bf16[32,16,128]{2,1,0:T(8,128)(2,1)} %pack.1), calls=%async_computation | async-start | bytes 262144 | tf_op jit(solution)/shard_map/all_to_all | solution.py:274
  21.5 0.7 copy-start.9
  22.2 0.7 copy-start.11
  33.8 0.7 copy-start.13
  34.5 0.6 copy-start.16
  35.1 0.6 copy-start.17
  35.7 17.2 %all-to-all-start.1 = ((bf16[24,16,256]{2,1,0:T(8,128)(2,1)}), bf16[24,16,256]{2,1,0:T(8,128)(2,1)S(1)}, u32[]{:S(2)}, u32[]{:S(2)}) async-start(bf16[24,16,256]{2,1,0:T(8,128)(2,1)} %get-tuple-element.17), calls=%async_computation.1 | async-start | bytes 393216 | tf_op jit(solution)/shard_map/all_to_all | solution.py:301
  47.8 0.9 copy-start.6
  52.8 1.1 %copy-start.7 = (bf16[8,192,256]{2,1,0:T(8,128)(2,1)S(1)}, bf16[8,192,256]{2,1,0:T(8,128)(2,1)}, u32[]{:S(2)}) copy-start(bf16[8,192,256]{2,1,0:T(8,128)(2,1)} %copy-done.6) | copy-start | bytes 2359300
  54.0 48.0 %copy-start.2 = (bf16[1280,640]{1,0:T(8,128)(2,1)S(1)}, bf16[1280,640]{1,0:T(8,128)(2,1)}, u32[]{:S(2)}) copy-start(bf16[1280,640]{1,0:T(8,128)(2,1)} %wout_ref.1) | copy-start | bytes 4915204
  56.1 0.7 copy-start.5
  56.7 45.2 %copy-start.1 = (bf16[640,1280]{1,0:T(8,128)(2,1)S(1)}, bf16[640,1280]{1,0:T(8,128)(2,1)}, u32[]{:S(2)}) copy-start(bf16[640,1280]{1,0:T(8,128)(2,1)} %win_ref.1) | copy-start | bytes 4915204
  56.7 20.5 %all-to-all-start.2 = ((bf16[24,16,256]{2,1,0:T(8,128)(2,1)}), bf16[24,16,256]{2,1,0:T(8,128)(2,1)S(1)}, u32[]{:S(2)}, u32[]{:S(2)}) async-start(bf16[24,16,256]{2,1,0:T(8,128)(2,1)} %copy-done.5), calls=%async_computation.2 | async-start | bytes 393216 | tf_op jit(solution)/shard_map/all_to_all | solution.py:314
  64.0 7.9 %collective-permute-start = (bf16[96,128]{1,0:T(8,128)(2,1)}, bf16[96,128]{1,0:T(8,128)(2,1)S(1)}, u32[]{:S(2)}, u32[]{:S(2)}) collective-permute-start(bf16[96,128]{1,0:T(8,128)(2,1)} %copy-done.17), channel_id=1, source_target_pairs={{0,32},{32,64},{64,96},{96,128},{128,160},{160,192},{192,224},{224... | collective-permute-start | bytes 73736 | tf_op jit(solution)/shard_map/ppermute | solution.py:303
  68.3 6.1 %collective-permute-start.1 = (bf16[96,128]{1,0:T(8,128)(2,1)}, bf16[96,128]{1,0:T(8,128)(2,1)}, u32[]{:S(2)}, u32[]{:S(2)}) collective-permute-start(bf16[96,128]{1,0:T(8,128)(2,1)} %copy-done.16), channel_id=1, source_target_pairs={{32,0},{64,32},{96,64},{128,96},{160,128},{192,160},{224,192},{256... | collective-permute-start | bytes 73736 | tf_op jit(solution)/shard_map/ppermute | solution.py:302
  74.4 0.9 copy-start.14
  76.5 0.8 copy-start.3
  77.2 1.0 copy-start.4
  78.2 1.0 copy-start.10
  79.2 1.0 copy-start.12
  80.9 0.7 copy-start.8
  81.6 20.4 %all-to-all-start.3 = ((bf16[32,16,128]{2,1,0:T(8,128)(2,1)}), bf16[32,16,128]{2,1,0:T(8,128)(2,1)S(1)}, u32[]{:S(2)}, u32[]{:S(2)}) async-start(bf16[32,16,128]{2,1,0:T(8,128)(2,1)} %copy-done.8), calls=%async_computation.3 | async-start | bytes 262144 | tf_op jit(solution)/shard_map/all_to_all | solution.py:336

commit v2 on v1

v2 whole, which is shorter than its diff:
```python
import math

import jax
import jax.numpy as jnp
from jax import lax
from jax.experimental import pallas as pl
from jax.experimental.pallas import tpu as pltpu
from jax.sharding import PartitionSpec as P

LON, LAT, COLS, ROWS, CHAN = 32, 24, 12, 8, 20
NLON, NLAT = LON * COLS, LAT * ROWS
PAIRS = COLS // 2
BF, F32 = jnp.bfloat16, jnp.float32
EPS = 1e-06
SLOTS = [*range(LAT // 2), *range(LAT - 1, LAT // 2 - 1, -1)]


def lanes_of(shape):
    return lax.broadcasted_iota(jnp.int32, shape, 1)


def inside(shape, start, width):
    lane = lanes_of(shape)
    return (lane >= start) & (lane < start + width)


def turn(x, shift):
    shift %= 128
    return x if shift == 0 else pltpu.roll(x, shift, 1)


VMEM, HBM, ANY, SMEM = pltpu.VMEM, pltpu.HBM, pl.ANY, pltpu.SMEM


def call(body, outs, args, scratch=(), name=None, mib=24, flops=0):
    result = pl.pallas_call(
        body,
        out_shape=[
            HBM(shape, kind) if space is HBM else jax.ShapeDtypeStruct(shape, kind) for shape, kind, space in outs
        ],
        in_specs=[pl.BlockSpec(memory_space=space) for _, space in args],
        out_specs=[pl.BlockSpec(memory_space=space) for _, _, space in outs],
        scratch_shapes=list(scratch),
        compiler_params=pltpu.CompilerParams(vmem_limit_bytes=mib * 2**20),
        cost_estimate=pl.CostEstimate(flops=flops, bytes_accessed=1_000_000, transcendentals=0),
        name=name,
    )(*(pltpu.with_memory_space_constraint(array, HBM) if space is HBM else array for array, space in args))
    return result[0] if len(outs) == 1 else result


def swap_halves(x):
    return pltpu.roll(x, LAT // 2, 0)


def begin(source, target, sem):
    copy = pltpu.make_async_copy(source, target, sem)
    copy.start()
    return copy


def pack_body(field_ref, out_ref, x_ref, send_ref, sems):
    shape = (16, 128)
    begin(field_ref, x_ref, sems.at[4]).wait()
    copies = []
    for d in range(LON):
        tile, off = divmod(CHAN * d, 128)
        last = (CHAN * d + CHAN - 1) // 128
        total = jnp.zeros(shape, F32)
        for q in range(PAIRS):
            at = slice(16 * q, 16 * q + 16)
            piece = x_ref[at, 128 * tile : 128 * tile + 128].astype(F32)
            if last > tile:
                after = x_ref[at, 128 * last : 128 * last + 128].astype(F32)
                piece = jnp.where(lanes_of(shape) >= off, piece, after)
            total = jnp.where(inside(shape, CHAN * q, CHAN), turn(piece, CHAN * q - off), total)
        send_ref[d] = total.astype(BF)
        if d % 8 == 7:
            at = pl.ds(d - 7, 8)
            copies.append(begin(send_ref.at[at], out_ref.at[at], sems.at[d // 8]))
    for copy in copies:
        copy.wait()


def wave(order, part, column):
    v = (order * column + part * (NLON // 4)).astype(F32)
    index = v - NLON * jnp.floor(v * (1.0 / NLON))
    x = (NLON // 4 - jnp.abs(index - NLON // 2)) * (2.0 * math.pi / NLON)
    y = x * x
    s = 1.0 / 6227020800.0
    for term in (-1.0 / 39916800.0, 1.0 / 362880.0, -1.0 / 5040.0, 1.0 / 120.0, -1.0 / 6.0, 1.0):
        s = s * y + term
    return -(s * x)


def mode_of(n):
    slot = n >> 4
    device = jnp.where(slot < LAT // 2, slot, LAT + LAT // 2 - 1 - slot)
    return (device << 3) + (n & 7), (n >> 3) & 1


def column_of(k):
    return COLS * (k & 31) + (k >> 5)


def halves(x):
    high = x.astype(BF)
    return high, (x - high.astype(F32)).astype(BF)


def fourier_body(sector_ref, kernel_ref, fhi_ref, flo_ref, taps_ref):
    shape = (16, NLON)
    lane = lanes_of(shape)

    def block(b, unused):
        row = lax.broadcasted_iota(jnp.int32, shape, 0) + 16 * b
        at = pl.ds(pl.multiple_of(16 * b, 16), 16)
        order, part = mode_of(row)
        table = wave(order, part, column_of(lane)) * (2.0 * math.pi / NLON)
        fhi_ref[at, :], flo_ref[at, :] = halves(table)
        return unused

    lax.fori_loop(0, NLON // 16, block, 0)
    wide = (kernel_ref.shape[1], 256)
    own = lanes_of(wide) & 31
    channel = lax.broadcasted_iota(jnp.int32, wide, 0)
    picked = (channel == own + sector_ref[0] * CHAN) & (own < CHAN)
    taps_ref[0:9, :] = jnp.dot(
        kernel_ref[...], jnp.where(picked, 1.0, 0.0), precision=lax.Precision.HIGHEST, preferred_element_type=F32
    )


def legendre_body(band_ref, p_out, pt_out, table, p_ref, pt_ref, sems):
    shape = (8, 128)
    lane = lanes_of(shape)
    order_i = lax.broadcasted_iota(jnp.int32, shape, 0) + band_ref[0] * 8
    order = order_i.astype(F32)
    r = jnp.floor((lane.astype(F32) + 0.5) * (1.0 / LAT))
    slot = lane.astype(F32) - LAT * r
    device = jnp.where(slot < LAT // 2, slot, LAT + LAT // 2 - 1.0 - slot)
    row = jnp.minimum(8.0 * device + r, NLAT - 1.0)
    theta = (row + 0.5) * (math.pi / NLAT)
    cosine, sine = jnp.cos(theta), jnp.sin(theta)
    k = lanes_of((8, 256)).astype(F32) + 1.0
    ratio = jnp.log((2.0 * k - 1.0) / (2.0 * k))
    factor = jnp.sum(jnp.where(k <= order[:, 0:1], ratio, 0.0), axis=1, keepdims=True)
    start = 0.5 * jnp.log((2.0 * order + 1.0) / (4.0 * math.pi)) + 0.5 * factor + order * jnp.log(sine)
    square = order * order
    every = 16

    def block(b, carry):
        before, current, log_scale = carry
        scale = jnp.exp(log_scale)
        for t in range(every):
            degree = b * every + t
            l = degree.astype(F32)
            lower = (l - 1.0) * (l - 1.0)
            alpha = jnp.sqrt((4.0 * l * l - 1.0) / jnp.maximum(l * l - square, 1.0))
            beta = jnp.sqrt(jnp.maximum(lower - square, 0.0) / jnp.maximum(4.0 * lower - 1.0, 1.0))
            fresh = (alpha * cosine) * current - (alpha * beta) * before
            fresh = jnp.where(order_i == degree, 1.0, fresh)
            fresh = jnp.where(order_i > degree, 0.0, fresh)
            before, current = current, fresh
            table[pl.ds(pl.multiple_of(degree * 8, 8), 8), :] = fresh * scale
        largest = jnp.maximum(jnp.abs(before), jnp.abs(current))
        largest = jnp.where(order_i <= b * every + (every - 1), largest, 1.0)
        return before / largest, current / largest, log_scale + jnp.log(largest)

    blank = jnp.zeros(shape, F32)
    lax.fori_loop(0, NLAT // every, block, (blank, blank, start))
    copies = []
    blank = jnp.zeros((128 - NLAT // 2, 128), F32)
    for m in range(8):
        for parity in range(2):
            p = jnp.where(lanes_of((96, 128)) < 96, table[pl.ds(8 * parity + m, 96, stride=16), :], 0.0)
            p_ref[m, 96 * parity : 96 * parity + 96, :] = p.astype(BF)
            turned = jnp.transpose(jnp.concatenate([p, blank], axis=0))
            pt_ref[m, 96 * parity : 96 * parity + 96, :] = turned[:96, :].astype(BF)
        if m % 4 == 3:
            at = pl.ds(m - 3, 4)
            copies.append(begin(p_ref.at[at], p_out.at[at], sems.at[m // 4]))
            copies.append(begin(pt_ref.at[at], pt_out.at[at], sems.at[2 + m // 4]))
    for copy in copies:
        copy.wait()


def spectrum_body(
    band_ref, recv_ref, fhi_ref, flo_ref, send_out, full_out, first_out, last_out, wide, full_ref, send_ref, edge_ref, sems
):
    wide[...] = recv_ref[...].astype(F32).reshape(LON * 16, 128)
    shape = (LON, 128)
    for e in range(2):
        for h in range(2):
            total = [jnp.zeros(shape, F32)] * PAIRS
            for s in range(4):
                rows = wide[pl.ds(8 * e + 4 * h + s, LON, stride=16), :]
                for q in range(PAIRS):
                    total[q] = jnp.where(inside(shape, 32 * s, CHAN), turn(rows, 32 * s - CHAN * q), total[q])
            for q in range(PAIRS):
                kap = 2 * q + e
                full_ref[32 * kap : 32 * kap + 32, 128 * h : 128 * h + 128] = total[q].astype(BF)
    copies = [begin(full_ref, full_out, sems.at[1])]
    full = full_ref[...]
    spectrum = jnp.dot(fhi_ref[...], full, preferred_element_type=F32)
    spectrum = spectrum + jnp.dot(flo_ref[...], full, preferred_element_type=F32)
    row = (lanes_of((1, 256)) >> 5) + band_ref[0] * ROWS
    weight = jnp.sin((row.astype(F32) + 0.5) * (math.pi / NLAT)) * (math.pi / NLAT)
    send_ref[...] = (spectrum * weight).astype(BF).reshape(LAT, 16, 256)
    copies.append(begin(send_ref, send_out, sems.at[0]))
    shape = (96, 128)
    for i, (edge_out, at, own) in enumerate(((first_out, 0, 0), (last_out, 128, 96))):
        edge = jnp.zeros(shape, F32)
        for g in range(4):
            rows = full_ref[96 * g : 96 * g + 96, at : at + 128].astype(F32)
            edge = jnp.where(inside(shape, 32 * g, 32), turn(rows, 32 * g - own), edge)
        edge_ref[i] = edge.astype(BF)
        copies.append(begin(edge_ref.at[i], edge_out, sems.at[2 + i]))
    for copy in copies:
        copy.wait()


def filter_body(recv_ref, p_in, pt_in, gain_in, send_out, wide, out, p_ref, pt_ref, gain_ref, send_ref, sems):
    cuts = [pl.ds(4 * i, 4) for i in range(2)]
    tables = []
    for i, at in enumerate(cuts):
        tables.append([begin(p_in.at[at], p_ref.at[at], sems.at[2 * i])])
        if i == 0:
            tables[0].append(begin(gain_in, gain_ref, sems.at[4]))
        tables[i].append(begin(pt_in.at[at], pt_ref.at[at], sems.at[2 * i + 1]))
    rows = LAT * 16
    for h in range(2):
        wide[rows * h : rows * h + rows, :] = recv_ref[:, :, 128 * h : 128 * h + 128].astype(F32).reshape(rows, 128)
    shape = (LAT, 128)
    lane = lanes_of(shape)
    blank = jnp.zeros((32, 128), F32)
    for m in range(8):
        chunks = []
        for h in range(2):
            low, high = (wide[pl.ds(rows * h + 8 * p + m, LAT, stride=16), :] for p in range(2))
            for s in range(4):
                chunks.append(jnp.where(lane < 32, turn(low, -32 * s), turn(high, 32 - 32 * s)))
        mirrored = [swap_halves(chunks[7 - r]) for r in range(4)]
        even = jnp.concatenate([chunks[r] + mirrored[r] for r in range(4)] + [blank], axis=0).astype(BF)
        odd = jnp.concatenate([chunks[r] - mirrored[r] for r in range(4)] + [blank], axis=0).astype(BF)
        if m % 4 == 0:
            for copy in tables[m // 4]:
                copy.wait()
        halves_back = []
        for parity in range(2):
            at = slice(96 * parity, 96 * parity + 96)
            field = even if (parity + m) % 2 == 0 else odd
            scaled = jnp.dot(p_ref[m, at, :], field, preferred_element_type=F32)
            scaled = scaled * gain_ref[pl.ds(parity, 96, stride=2), :]
            scaled = jnp.concatenate([scaled, blank], axis=0).astype(BF)
            halves_back.append(jnp.dot(pt_ref[m, at, :], scaled, preferred_element_type=F32))
        if m % 2 == 1:
            halves_back.reverse()
        near, far = halves_back[0] + halves_back[1], halves_back[0] - halves_back[1]
        back = [near[LAT * r : LAT * r + LAT, :] for r in range(4)]
        back = back + [swap_halves(far[LAT * r : LAT * r + LAT, :]) for r in (3, 2, 1, 0)]
        for p in range(2):
            for h in range(2):
                total = jnp.zeros(shape, F32)
                for s in range(4):
                    r = 4 * h + s
                    total = jnp.where(
                        inside(shape, 32 * s, 32), turn(back[r], 32 * s - 32 * p), total
                    )
                out[pl.ds(rows * h + 8 * p + m, LAT, stride=16), :] = total
    for h in range(2):
        send_ref[:, :, 128 * h : 128 * h + 128] = out[rows * h : rows * h + rows, :].astype(BF).reshape(LAT, 16, 128)
    begin(send_ref, send_out, sems.at[5]).wait()


def local_body(full_in, above_ref, below_ref, taps_ref, base_out, full_ref, base_ref, up, down, sems):
    begin(full_in, full_ref, sems.at[0]).wait()
    shape = (96, 128)
    lane = lanes_of(shape)
    for g in range(4):
        at = slice(96 * g, 96 * g + 96)
        left, right = full_ref[at, 0:128].astype(F32), full_ref[at, 128:256].astype(F32)
        above, below = above_ref[...].astype(F32), below_ref[...].astype(F32)
        up[at, 0:128] = jnp.where(lane < 32, turn(above, -32 * g), turn(left, 32))
        up[at, 128:256] = jnp.where(lane < 32, turn(left, 32), turn(right, 32))
        down[at, 0:128] = jnp.where(lane >= 96, turn(right, 96), turn(left, 96))
        down[at, 128:256] = jnp.where(lane >= 96, turn(below, 96 - 32 * g), turn(right, 96))

    def mixed(kap, b):
        at = slice(32 * kap, 32 * kap + 32)
        rows = (up[at, :], full_ref[at, :].astype(F32), down[at, :])
        return sum(taps_ref[3 * i + b : 3 * i + b + 1, :] * rows[i] for i in range(3))

    for kap in range(COLS):
        west = mixed(kap - 1, 0) if kap > 0 else pltpu.roll(mixed(COLS - 1, 0), 1, 0)
        east = mixed(kap + 1, 2) if kap < COLS - 1 else pltpu.roll(mixed(0, 2), LON - 1, 0)
        at = slice(32 * kap, 32 * kap + 32)
        base_ref[at, :] = (full_ref[at, :].astype(F32) + (west + mixed(kap, 1) + east)).astype(BF)
    begin(base_ref, base_out, sems.at[1]).wait()


def synthesis_body(recv_ref, base_in, send_out, inv_ref, base_ref, send_ref, out, summed_ref, sems):
    base = begin(base_in, base_ref, sems.at[0])
    shape = (LON, NLON)
    order, part = mode_of(lanes_of(shape))
    column = COLS * lax.broadcasted_iota(jnp.int32, shape, 0)
    weight = jnp.where(order == 0, 1.0, 2.0)
    cosine, sine = wave(order, part, column) * weight, wave(order, part + 1, column) * weight
    shape = (16, NLON)
    order, _ = mode_of(lanes_of(shape))
    column = lax.broadcasted_iota(jnp.int32, shape, 0)
    step_cosine, step_sine = wave(order, 0, column), wave(order, 1, column)
    for kap in range(COLS):
        turned = cosine * step_cosine[kap : kap + 1, :] - sine * step_sine[kap : kap + 1, :]
        inv_ref[32 * kap : 32 * kap + 32, :] = turned.astype(BF)
    summed_ref[...] = jnp.dot(inv_ref[...], recv_ref[...].reshape(NLON, 256), preferred_element_type=F32)
    base.wait()
    summed_ref[...] += base_ref[...].astype(F32)
    shape = (LON, 128)
    for e in range(2):
        for h in range(2):
            for s in range(4):
                total = jnp.zeros(shape, F32)
                for q in range(PAIRS):
                    kap = 2 * q + e
                    rows = summed_ref[32 * kap : 32 * kap + 32, 128 * h : 128 * h + 128]
                    total = jnp.where(inside(shape, CHAN * q, CHAN), turn(rows, CHAN * q - 32 * s), total)
                out[pl.ds(8 * e + 4 * h + s, LON, stride=16), :] = total
    send_ref[...] = out[...].astype(BF).reshape(LON, 16, 128)
    begin(send_ref, send_out, sems.at[1]).wait()


def mlp_body(recv_ref, gain_ref, win_ref, wout_ref, out_ref, summed_ref):
    shape = (16, 128)
    lane = lanes_of(shape)
    for tile in range(5):
        for q in range(PAIRS):
            total = jnp.zeros(shape, F32)
            for d in range(128 * tile // CHAN, (128 * tile + 127) // CHAN + 1):
                off = CHAN * d - 128 * tile
                piece = turn(recv_ref[d].astype(F32), off - CHAN * q)
                total = jnp.where((lane >= off) & (lane < off + CHAN), piece, total)
            summed_ref[16 * q : 16 * q + 16, 128 * tile : 128 * tile + 128] = total
    summed = summed_ref[...]
    mean = jnp.sum(summed * summed, axis=1, keepdims=True) * (1.0 / summed.shape[1])
    normed = (summed * lax.rsqrt(mean + EPS) * gain_ref[...]).astype(BF)
    hidden = jnp.dot(normed, win_ref[...], preferred_element_type=F32)
    hidden = (0.5 * hidden * (1.0 + lax.erf(hidden * math.sqrt(0.5)))).astype(BF)
    result = summed + jnp.dot(hidden, wout_ref[...], preferred_element_type=F32)
    out_ref[...] = result.astype(BF)


def on_device(latent_field, spectral_filter, conv_weight, norm_gain, weight_in, weight_out):
    channels = latent_field.shape[0]
    points = COLS * ROWS
    table, circle, group, mode = (NLON, NLON), (NLON, 256), (LON, 16, 128), (LAT, 16, 256)
    field = jnp.transpose(latent_field, (2, 1, 0)).reshape(points, channels)
    pieces = call(
        pack_body,
        [(group, BF, HBM)],
        [(field, HBM)],
        [VMEM((points, channels), BF), VMEM(group, BF), pltpu.SemaphoreType.DMA((5,))],
        name="pack",
    )
    pieces = lax.all_to_all(pieces, "lon", 0, 0, tiled=True)

    sector = lax.axis_index("lon").astype(jnp.int32).reshape(1)
    band = lax.axis_index("lat").astype(jnp.int32).reshape(1)
    fhi, flo, taps = call(
        fourier_body,
        [(table, BF, VMEM), (table, BF, VMEM), ((16, 256), F32, VMEM)],
        [(sector, SMEM), (conv_weight, VMEM)],
        name="fourier_tables",
        flops=10_000_000,
    )
    modes, full, first, last = call(
        spectrum_body,
        [(mode, BF, HBM), (circle, BF, HBM), ((96, 128), BF, HBM), ((96, 128), BF, HBM)],
        [(band, SMEM), (pieces, VMEM), (fhi, VMEM), (flo, VMEM)],
        [VMEM((LON * 16, 128), F32), VMEM(circle, BF), VMEM(mode, BF), VMEM((2, 96, 128), BF), pltpu.SemaphoreType.DMA((4,))],
        name="spectrum",
    )
    modes = lax.all_to_all(modes, "lat", 0, 0, tiled=True, axis_index_groups=[SLOTS])
    polynomials = (8, NLAT, 128)
    p, pt = call(
        legendre_body,
        [(polynomials, BF, HBM)] * 2,
        [(band, SMEM)],
        [VMEM((NLAT * 8, 128), F32), VMEM(polynomials, BF), VMEM(polynomials, BF), pltpu.SemaphoreType.DMA((4,))],
        name="legendre_tables",
        flops=10_000_000,
    )
    gain = jnp.tile(jnp.pad(jnp.transpose(spectral_filter), ((0, 0), (0, 32 - CHAN))), (1, 4))
    modes = call(
        filter_body,
        [(mode, BF, HBM)],
        [(modes, VMEM), (p, HBM), (pt, HBM), (gain, HBM)],
        [VMEM((2 * LAT * 16, 128), F32)] * 2
        + [VMEM(polynomials, BF)] * 2
        + [VMEM((NLAT, 128), F32), VMEM(mode, BF), pltpu.SemaphoreType.DMA((6,))],
        name="filter",
    )
    modes = lax.all_to_all(modes, "lat", 0, 0, tiled=True, axis_index_groups=[SLOTS])
    below = lax.ppermute(first, "lat", [(i + 1, i) for i in range(LAT - 1)])
    above = lax.ppermute(last, "lat", [(i, i + 1) for i in range(LAT - 1)])
    base = call(
        local_body,
        [(circle, BF, HBM)],
        [(full, HBM), (above, VMEM), (below, VMEM), (taps, VMEM)],
        [VMEM(circle, BF)] * 2 + [VMEM(circle, F32)] * 2 + [pltpu.SemaphoreType.DMA((2,))],
        name="local_mix",
        flops=5_000_000,
    )
    pieces = call(
        synthesis_body,
        [(group, BF, HBM)],
        [(modes, VMEM), (base, HBM)],
        [VMEM(table, BF), VMEM(circle, BF), VMEM(group, BF), VMEM((LON * 16, 128), F32), VMEM(circle, F32)]
        + [pltpu.SemaphoreType.DMA((2,))],
        name="synthesis",
    )
    pieces = lax.all_to_all(pieces, "lon", 0, 0, tiled=True)
    result = call(
        mlp_body,
        [((points, channels), BF, VMEM)],
        [(pieces, VMEM), (norm_gain.reshape(1, channels), VMEM), (weight_in, VMEM), (weight_out, VMEM)],
        [VMEM((points, channels), F32)],
        name="mlp",
    )
    return jnp.transpose(result.reshape(COLS, ROWS, channels), (2, 1, 0))


def solution(mesh):
    in_specs = (P(None, "lat", "lon"), P("lon", None), P(), P(), P(), P())
    return jax.shard_map(on_device, mesh=mesh, in_specs=in_specs, out_specs=P(None, "lat", "lon"), check_vma=False)
```

time: 104 us -> 98.3 us (0.945)
  local copies, waits for them, and re-layouts: 14.6 us -> 3.24 us
  Pallas kernels: 11.7 us -> 15.9 us
  waiting for transfers between devices: 28.3 us -> 29.7 us
    unnamed x38 -> x14, local copies, waits for them, and re-layouts: 12.2 us -> 0.8 us
    pallas_call x8, Pallas kernels: 11.7 us -> 15.9 us  [call(): pl.pallas_call(body, out_shape=[HBM(shape, kind) if space is HBM else jax...]
    all_to_all x2, waiting for transfers between devices: 4.16 us -> 2.47 us  [on_device(): lax.all_to_all(modes, 'lat', 0, 0, tiled=True, axis_index_groups=[SLOTS])]
    all_to_all x2, waiting for transfers between devices: 21.7 us -> 23.3 us  [on_device(): pieces = lax.all_to_all(pieces, 'lon', 0, 0, tiled=True)]
    ppermute x1, waiting for transfers between devices: 2.5 us -> 3.72 us  [on_device(): below = lax.ppermute(first, 'lat', [(i + 1, i) for i in range(LAT - 1)])]
    another operation x4 -> x2, local copies, waits for them, and re-layouts: 1.66 us -> 2.43 us  [on_device(): jnp.tile(jnp.pad(jnp.transpose(spectral_filter), ((0, 0), (0, 32 - CHAN))...]
  transfers between devices with their start and end apart: 6 -> 6, of which waited for: 4 -> 5; matrix products, arithmetic and copies ran while one was open for 2% -> 2% of each run, Pallas kernels for 5% -> 6%
where the time goes in v2:
time: 98.3 us; the launch traced here: 97.7 us
  starting transfers between devices  48.7 us (50%)
  waiting for transfers between devices  29.7 us (30%)
  Pallas kernels  15.9 us (16%)
  local copies, waits for them, and re-layouts  3.24 us (3%)
    all_to_all x2, starting transfers between devices, on_device(): pieces = lax.all_to_all(pieces, 'lon', 0, 0, tiled=True)  25.4 us
    all_to_all x2, waiting for transfers between devices, on_device(): pieces = lax.all_to_all(pieces, 'lon', 0, 0, tiled=True)  23.3 us
    all_to_all x2, starting transfers between devices, on_device(): lax.all_to_all(modes, 'lat', 0, 0, tiled=True, axis_index_groups=[SLOTS])  17.1 us
    pallas_call x8, Pallas kernels, call(): pl.pallas_call(body, out_shape=[HBM(shape, kind) if space is HBM else jax...  15.9 us
    ppermute x1, starting transfers between devices, on_device(): above = lax.ppermute(last, 'lat', [(i, i + 1) for i in range(LAT - 1)])  4.3 us
    ppermute x1, waiting for transfers between devices, on_device(): below = lax.ppermute(first, 'lat', [(i + 1, i) for i in range(LAT - 1)])  3.72 us
    all_to_all x2, waiting for transfers between devices, on_device(): lax.all_to_all(modes, 'lat', 0, 0, tiled=True, axis_index_groups=[SLOTS])  2.47 us
    another operation x2, local copies, waits for them, and re-layouts, on_device(): jnp.tile(jnp.pad(jnp.transpose(spectral_filter), ((0, 0), (0, 32 - CHAN))...  2.43 us
  transfers between devices with their start and end apart: 6, of which 5 were waited for; matrix products, arithmetic and copies ran while one was open for 2% of the time, Pallas kernels for 6%

profile of v2, /device:TPU:25, one launch (start us, length us, event | category | flops | bytes accessed | tf_op | source)
XLA Modules:
  0.0 97.7 jit_solution(4457607990315713431)
XLA Ops:
  0.0 1.8 %pack.1 = bf16[32,16,128]{2,1,0:T(8,128)(2,1)} custom-call(bf16[96,640]{1,0:T(8,128)(2,1)} %bitcast.11), custom_call_target="tpu_custom_call" | custom-call | bytes 1000000 | tf_op jit(solution)/shard_map/pack/pallas_call | solution.py:36
  1.8 17.8 %all-to-all-start = ((bf16[32,16,128]{2,1,0:T(8,128)(2,1)}), bf16[32,16,128]{2,1,0:T(8,128)(2,1)S(1)}, u32[]{:S(2)}, u32[]{:S(2)}) async-start(bf16[32,16,128]{2,1,0:T(8,128)(2,1)} %pack.1), calls=%async_computation | async-start | bytes 262144 | tf_op jit(solution)/shard_map/all_to_all | solution.py:363
  19.7 0.0 copy-start.2
  19.7 0.8 copy-done.2
  20.4 1.5 %fourier_tables.1 = (bf16[384,384]{1,0:T(8,128)(2,1)S(1)}, bf16[384,384]{1,0:T(8,128)(2,1)S(1)}, f32[16,256]{1,0:T(8,128)S(1)}) custom-call(s32[1]{0:T(128)} %bitcast.3.sector_ref, f32[9,640]{1,0:T(8,128)S(1)} %copy-done.2), custom_call_target="tpu_custom_call" | custom-call | flops 10000000 | bytes 1000000 | tf_op jit(solution)/shard_map/fourier_tables/pallas_call | solution.py:36
  21.9 10.6 %all-to-all-done.recv_ref = bf16[32,16,128]{2,1,0:T(8,128)(2,1)S(1)} async-done(((bf16[32,16,128]{2,1,0:T(8,128)(2,1)}), bf16[32,16,128]{2,1,0:T(8,128)(2,1)S(1)}, u32[]{:S(2)}, u32[]{:S(2)}) %all-to-all-start) | async-done | bytes 131104 | tf_op jit(solution)/shard_map/all_to_all | solution.py:363
  32.5 1.4 %spectrum.1 = (bf16[24,16,256]{2,1,0:T(8,128)(2,1)}, bf16[384,256]{1,0:T(8,128)(2,1)}, bf16[96,128]{1,0:T(8,128)(2,1)}, bf16[96,128]{1,0:T(8,128)(2,1)}) custom-call(s32[1]{0:T(128)} %bitcast.band_ref, bf16[32,16,128]{2,1,0:T(8,128)(2,1)S(1)} %all-to-all-done.recv_ref, bf16[384,384]{1,0:T(8,128)(2,1)S(1)} %get-tuple-element.14.fhi_ref, ...), custom_call_target="tpu_custom_call" | custom-call | bytes 1000000 | tf_op jit(solution)/shard_map/spectrum/pallas_call | solution.py:36
  33.9 0.0 copy-start.6
  33.9 0.0 copy-start.5
  33.9 10.1 %all-to-all-start.1 = ((bf16[24,16,256]{2,1,0:T(8,128)(2,1)}), bf16[24,16,256]{2,1,0:T(8,128)(2,1)S(1)}, u32[]{:S(2)}, u32[]{:S(2)}) async-start(bf16[24,16,256]{2,1,0:T(8,128)(2,1)} %get-tuple-element.16), calls=%async_computation.1 | async-start | bytes 393216 | tf_op jit(solution)/shard_map/all_to_all | solution.py:381
  44.0 0.0 copy-done.3
  44.0 0.0 copy-start.1
  44.0 0.7 tile.4
  44.7 1.8 %copy.8.gain_in = f32[192,128]{1,0:T(8,128)} copy(f32[192,128]{0,1:T(8,128)} %bitcast.10) | data formatting | bytes 196608 | tf_op jit(solution)/shard_map/tile | solution.py:391
  46.5 2.4 %legendre_tables.1 = (bf16[8,192,128]{2,1,0:T(8,128)(2,1)}, bf16[8,192,128]{2,1,0:T(8,128)(2,1)}) custom-call(s32[1]{0:T(128)} %bitcast.band_ref), custom_call_target="tpu_custom_call" | custom-call | flops 10000000 | bytes 1000000 | tf_op jit(solution)/shard_map/legendre_tables/pallas_call | solution.py:36
  48.8 2.5 %all-to-all-done.1.recv_ref = bf16[24,16,256]{2,1,0:T(8,128)(2,1)S(1)} async-done(((bf16[24,16,256]{2,1,0:T(8,128)(2,1)}), bf16[24,16,256]{2,1,0:T(8,128)(2,1)S(1)}, u32[]{:S(2)}, u32[]{:S(2)}) %all-to-all-start.1) | async-done | bytes 196640 | tf_op jit(solution)/shard_map/all_to_all | solution.py:381
  51.3 3.0 %filter.1 = bf16[24,16,256]{2,1,0:T(8,128)(2,1)} custom-call(bf16[24,16,256]{2,1,0:T(8,128)(2,1)S(1)} %all-to-all-done.1.recv_ref, bf16[8,192,128]{2,1,0:T(8,128)(2,1)} %get-tuple-element.17.p_in, bf16[8,192,128]{2,1,0:T(8,128)(2,1)} %get-tuple-element.18.pt_in, f32[192,128]{1,0:T(8,128)} %copy.8.gain_in), custom_call_target="tpu_custom_call" | custom-call | bytes 1000000 | tf_op jit(solution)/shard_map/filter/pallas_call | solution.py:36
  54.3 7.0 %all-to-all-start.2 = ((bf16[24,16,256]{2,1,0:T(8,128)(2,1)}), bf16[24,16,256]{2,1,0:T(8,128)(2,1)S(1)}, u32[]{:S(2)}, u32[]{:S(2)}) async-start(bf16[24,16,256]{2,1,0:T(8,128)(2,1)} %filter.1), calls=%async_computation.2 | async-start | bytes 393216 | tf_op jit(solution)/shard_map/all_to_all | solution.py:401
  61.3 0.0 copy-done.6
  61.3 4.3 %collective-permute-start = (bf16[96,128]{1,0:T(8,128)(2,1)S(1)}, bf16[96,128]{1,0:T(8,128)(2,1)S(1)}, u32[]{:S(2)}, u32[]{:S(2)}) collective-permute-start(bf16[96,128]{1,0:T(8,128)(2,1)S(1)} %copy-done.6), channel_id=1, source_target_pairs={{0,32},{32,64},{64,96},{96,128},{128,160},{160,192},{192,224},{224... | collective-permute-start | bytes 73736 | tf_op jit(solution)/shard_map/ppermute | solution.py:403
  65.6 0.0 copy-done.5
  65.6 1.9 %collective-permute-start.1 = (bf16[96,128]{1,0:T(8,128)(2,1)S(1)}, bf16[96,128]{1,0:T(8,128)(2,1)S(1)}, u32[]{:S(2)}, u32[]{:S(2)}) collective-permute-start(bf16[96,128]{1,0:T(8,128)(2,1)S(1)} %copy-done.5), channel_id=1, source_target_pairs={{32,0},{64,32},{96,64},{128,96},{160,128},{192,160},{224,192},{256... | collective-permute-start | bytes 73736 | tf_op jit(solution)/shard_map/ppermute | solution.py:402
  67.6 0.1 collective-permute-done.above_ref
  67.7 3.7 %collective-permute-done.1.below_ref = bf16[96,128]{1,0:T(8,128)(2,1)S(1)} collective-permute-done((bf16[96,128]{1,0:T(8,128)(2,1)S(1)}, bf16[96,128]{1,0:T(8,128)(2,1)S(1)}, u32[]{:S(2)}, u32[]{:S(2)}) %collective-permute-start.1) | collective-permute-done | bytes 24608 | tf_op jit(solution)/shard_map/ppermute | solution.py:402
  71.4 2.0 %local_mix.1.base_in = bf16[384,256]{1,0:T(8,128)(2,1)} custom-call(bf16[384,256]{1,0:T(8,128)(2,1)} %get-tuple-element.19.full_in, bf16[96,128]{1,0:T(8,128)(2,1)S(1)} %collective-permute-done.above_ref, bf16[96,128]{1,0:T(8,128)(2,1)S(1)} %collective-permute-done.1.below_ref, f32[16,256]{1,0:T(8,128)S(1)} %get-tuple-element.22.taps_ref), custom_call_target="tpu_custom_call" | custom-call | flops 5000000 | bytes 1000000 | tf_op jit(solution)/shard_map/local_mix/pallas_call | solution.py:36
  73.4 0.0 all-to-all-done.2.recv_ref
  73.5 2.1 %synthesis.1 = bf16[32,16,128]{2,1,0:T(8,128)(2,1)} custom-call(bf16[24,16,256]{2,1,0:T(8,128)(2,1)S(1)} %all-to-all-done.2.recv_ref, bf16[384,256]{1,0:T(8,128)(2,1)} %local_mix.1.base_in), custom_call_target="tpu_custom_call" | custom-call | bytes 1000000 | tf_op jit(solution)/shard_map/synthesis/pallas_call | solution.py:36
  75.6 7.6 %all-to-all-start.3 = ((bf16[32,16,128]{2,1,0:T(8,128)(2,1)}), bf16[32,16,128]{2,1,0:T(8,128)(2,1)S(1)}, u32[]{:S(2)}, u32[]{:S(2)}) async-start(bf16[32,16,128]{2,1,0:T(8,128)(2,1)} %synthesis.1), calls=%async_computation.3 | async-start | bytes 262144 | tf_op jit(solution)/shard_map/all_to_all | solution.py:420
  83.2 0.0 copy-done.4
  83.2 12.8 %all-to-all-done.3.recv_ref = bf16[32,16,128]{2,1,0:T(8,128)(2,1)S(1)} async-done(((bf16[32,16,128]{2,1,0:T(8,128)(2,1)}), bf16[32,16,128]{2,1,0:T(8,128)(2,1)S(1)}, u32[]{:S(2)}, u32[]{:S(2)}) %all-to-all-start.3) | async-done | bytes 131104 | tf_op jit(solution)/shard_map/all_to_all | solution.py:420
  96.0 0.0 copy-done.1
  96.0 1.7 %mlp.1 = bf16[96,640]{1,0:T(8,128)(2,1)} custom-call(bf16[32,16,128]{2,1,0:T(8,128)(2,1)S(1)} %all-to-all-done.3.recv_ref, f32[1,640]{1,0:T(1,128)S(1)} %reshape.22.gain_ref, bf16[640,1280]{1,0:T(8,128)(2,1)S(1)} %copy-done, bf16[1280,640]{1,0:T(8,128)(2,1)S(1)} %copy-done.1), custom_call_target="tpu_custom_call" | custom-call | bytes 1000000 | tf_op jit(solution)/shard_map/mlp/pallas_call | solution.py:36
  (6 shorter events, 0.0 us)
Async XLA Ops:
  0.0 44.0 %copy-start.3 = (f32[20,192]{1,0:T(8,128)S(1)}, f32[20,192]{1,0:T(8,128)}, u32[]{:S(2)}) copy-start(f32[20,192]{1,0:T(8,128)} %param.7) | copy-start | bytes 46084
  1.8 30.6 %all-to-all-start = ((bf16[32,16,128]{2,1,0:T(8,128)(2,1)}), bf16[32,16,128]{2,1,0:T(8,128)(2,1)S(1)}, u32[]{:S(2)}, u32[]{:S(2)}) async-start(bf16[32,16,128]{2,1,0:T(8,128)(2,1)} %pack.1), calls=%async_computation | async-start | bytes 262144 | tf_op jit(solution)/shard_map/all_to_all | solution.py:363
  19.7 0.8 copy-start.2
  33.9 27.4 %copy-start.6 = (bf16[96,128]{1,0:T(8,128)(2,1)S(1)}, bf16[96,128]{1,0:T(8,128)(2,1)}, u32[]{:S(2)}) copy-start(bf16[96,128]{1,0:T(8,128)(2,1)} %get-tuple-element.20) | copy-start | bytes 73732
  33.9 31.8 %copy-start.5 = (bf16[96,128]{1,0:T(8,128)(2,1)S(1)}, bf16[96,128]{1,0:T(8,128)(2,1)}, u32[]{:S(2)}) copy-start(bf16[96,128]{1,0:T(8,128)(2,1)} %get-tuple-element.21) | copy-start | bytes 73732
  33.9 17.4 %all-to-all-start.1 = ((bf16[24,16,256]{2,1,0:T(8,128)(2,1)}), bf16[24,16,256]{2,1,0:T(8,128)(2,1)S(1)}, u32[]{:S(2)}, u32[]{:S(2)}) async-start(bf16[24,16,256]{2,1,0:T(8,128)(2,1)} %get-tuple-element.16), calls=%async_computation.1 | async-start | bytes 393216 | tf_op jit(solution)/shard_map/all_to_all | solution.py:381
  44.0 52.0 %copy-start.1 = (bf16[1280,640]{1,0:T(8,128)(2,1)S(1)}, bf16[1280,640]{1,0:T(8,128)(2,1)}, u32[]{:S(2)}) copy-start(bf16[1280,640]{1,0:T(8,128)(2,1)} %wout_ref.1) | copy-start | bytes 4915204
  44.7 38.5 %copy-start.4 = (f32[640]{0:T(1024)S(1)}, f32[640]{0:T(1024)}, u32[]{:S(2)}) copy-start(f32[640]{0:T(1024)} %param.9) | copy-start | bytes 7684
  44.7 51.3 %copy-start = (bf16[640,1280]{1,0:T(8,128)(2,1)S(1)}, bf16[640,1280]{1,0:T(8,128)(2,1)}, u32[]{:S(2)}) copy-start(bf16[640,1280]{1,0:T(8,128)(2,1)} %win_ref.1) | copy-start | bytes 4915204
  54.3 19.1 %all-to-all-start.2 = ((bf16[24,16,256]{2,1,0:T(8,128)(2,1)}), bf16[24,16,256]{2,1,0:T(8,128)(2,1)S(1)}, u32[]{:S(2)}, u32[]{:S(2)}) async-start(bf16[24,16,256]{2,1,0:T(8,128)(2,1)} %filter.1), calls=%async_computation.2 | async-start | bytes 393216 | tf_op jit(solution)/shard_map/all_to_all | solution.py:401
  61.3 6.4 %collective-permute-start = (bf16[96,128]{1,0:T(8,128)(2,1)S(1)}, bf16[96,128]{1,0:T(8,128)(2,1)S(1)}, u32[]{:S(2)}, u32[]{:S(2)}) collective-permute-start(bf16[96,128]{1,0:T(8,128)(2,1)S(1)} %copy-done.6), channel_id=1, source_target_pairs={{0,32},{32,64},{64,96},{96,128},{128,160},{160,192},{192,224},{224... | collective-permute-start | bytes 73736 | tf_op jit(solution)/shard_map/ppermute | solution.py:403
  65.6 5.8 %collective-permute-start.1 = (bf16[96,128]{1,0:T(8,128)(2,1)S(1)}, bf16[96,128]{1,0:T(8,128)(2,1)S(1)}, u32[]{:S(2)}, u32[]{:S(2)}) collective-permute-start(bf16[96,128]{1,0:T(8,128)(2,1)S(1)} %copy-done.5), channel_id=1, source_target_pairs={{32,0},{64,32},{96,64},{128,96},{160,128},{192,160},{224,192},{256... | collective-permute-start | bytes 73736 | tf_op jit(solution)/shard_map/ppermute | solution.py:402
  75.6 20.4 %all-to-all-start.3 = ((bf16[32,16,128]{2,1,0:T(8,128)(2,1)}), bf16[32,16,128]{2,1,0:T(8,128)(2,1)S(1)}, u32[]{:S(2)}, u32[]{:S(2)}) async-start(bf16[32,16,128]{2,1,0:T(8,128)(2,1)} %synthesis.1), calls=%async_computation.3 | async-start | bytes 262144 | tf_op jit(solution)/shard_map/all_to_all | solution.py:420

commit v3 on v2

--- a/solution.py
+++ b/solution.py
@@ -95,7 +95,9 @@
 def mode_of(n):
     slot = n >> 4
     device = jnp.where(slot < LAT // 2, slot, LAT + LAT // 2 - 1 - slot)
-    return (device << 3) + (n & 7), (n >> 3) & 1
+    order, part = (device << 3) + (n & 7), (n >> 3) & 1
+    highest = (order == 0) & (part == 1)
+    return jnp.where(highest, NLON // 2, order), jnp.where(highest, 0, part)
 
 
 def column_of(k):
@@ -107,7 +109,8 @@
     return high, (x - high.astype(F32)).astype(BF)
 
 
-def fourier_body(sector_ref, kernel_ref, fhi_ref, flo_ref, taps_ref):
+def fourier_body(sector_ref, kernel_in, fhi_ref, flo_ref, taps_ref, kernel_ref, sem):
+    arriving = begin(kernel_in, kernel_ref, sem)
     shape = (16, NLON)
     lane = lanes_of(shape)
 
@@ -120,6 +123,7 @@
         return unused
 
     lax.fori_loop(0, NLON // 16, block, 0)
+    arriving.wait()
     wide = (kernel_ref.shape[1], 256)
     own = lanes_of(wide) & 31
     channel = lax.broadcasted_iota(jnp.int32, wide, 0)
@@ -129,7 +133,10 @@
     )
 
 
-def legendre_body(band_ref, p_out, pt_out, table, p_ref, pt_ref, sems):
+def legendre_body(
+    band_ref, gain_in, p_out, pt_out, gain_out, table, p_ref, pt_ref, gain_ref, own_ref, square_ref, sems
+):
+    arriving = begin(gain_in, own_ref, sems.at[4])
     shape = (8, 128)
     lane = lanes_of(shape)
     order_i = lax.broadcasted_iota(jnp.int32, shape, 0) + band_ref[0] * 8
@@ -168,11 +175,20 @@
     blank = jnp.zeros(shape, F32)
     lax.fori_loop(0, NLAT // every, block, (blank, blank, start))
     copies = []
+    arriving.wait()
+    square_ref[0:CHAN, 0:NLAT] = own_ref[...]
+    for h in range(2):
+        piece = jnp.transpose(square_ref[:, 128 * h : 128 * h + 128])
+        piece = jnp.where(lanes_of((128, 128)) < CHAN, piece, 0.0)
+        height = 128 if h == 0 else NLAT - 128
+        gain_ref[128 * h : 128 * h + height, :] = (piece + turn(piece, 32))[:height, :]
+    copies.append(begin(gain_ref, gain_out, sems.at[5]))
+    weight = sine[0:1, :] * (math.pi / NLAT)
     blank = jnp.zeros((128 - NLAT // 2, 128), F32)
     for m in range(8):
         for parity in range(2):
             p = jnp.where(lanes_of((96, 128)) < 96, table[pl.ds(8 * parity + m, 96, stride=16), :], 0.0)
-            p_ref[m, 96 * parity : 96 * parity + 96, :] = p.astype(BF)
+            p_ref[m, 96 * parity : 96 * parity + 96, :] = (p * weight).astype(BF)
             turned = jnp.transpose(jnp.concatenate([p, blank], axis=0))
             pt_ref[m, 96 * parity : 96 * parity + 96, :] = turned[:96, :].astype(BF)
         if m % 4 == 3:
@@ -183,9 +199,7 @@
         copy.wait()
 
 
-def spectrum_body(
-    band_ref, recv_ref, fhi_ref, flo_ref, send_out, full_out, first_out, last_out, wide, full_ref, send_ref, edge_ref, sems
-):
+def spectrum_body(recv_ref, fhi_ref, flo_ref, unused_a, unused_b, send_out, full_out, wide, full_ref, send_ref, sems):
     wide[...] = recv_ref[...].astype(F32).reshape(LON * 16, 128)
     shape = (LON, 128)
     for e in range(2):
@@ -202,23 +216,29 @@
     full = full_ref[...]
     spectrum = jnp.dot(fhi_ref[...], full, preferred_element_type=F32)
     spectrum = spectrum + jnp.dot(flo_ref[...], full, preferred_element_type=F32)
-    row = (lanes_of((1, 256)) >> 5) + band_ref[0] * ROWS
-    weight = jnp.sin((row.astype(F32) + 0.5) * (math.pi / NLAT)) * (math.pi / NLAT)
-    send_ref[...] = (spectrum * weight).astype(BF).reshape(LAT, 16, 256)
+    send_ref[...] = spectrum.astype(BF).reshape(LAT, 16, 256)
     copies.append(begin(send_ref, send_out, sems.at[0]))
-    shape = (96, 128)
-    for i, (edge_out, at, own) in enumerate(((first_out, 0, 0), (last_out, 128, 96))):
-        edge = jnp.zeros(shape, F32)
-        for g in range(4):
-            rows = full_ref[96 * g : 96 * g + 96, at : at + 128].astype(F32)
-            edge = jnp.where(inside(shape, 32 * g, 32), turn(rows, 32 * g - own), edge)
-        edge_ref[i] = edge.astype(BF)
-        copies.append(begin(edge_ref.at[i], edge_out, sems.at[2 + i]))
     for copy in copies:
         copy.wait()
 
 
-def filter_body(recv_ref, p_in, pt_in, gain_in, send_out, wide, out, p_ref, pt_ref, gain_ref, send_ref, sems):
+def row_after(x):
+    slot = lax.broadcasted_iota(jnp.int32, x.shape, 0)
+    half = LAT // 2
+    moved = jnp.where(slot < half - 1, pltpu.roll(x, LAT - 1, 0), pltpu.roll(x, 1, 0))
+    return jnp.where(slot == half - 1, swap_halves(x), jnp.where(slot == half, 0.0, moved))
+
+
+def row_before(x):
+    slot = lax.broadcasted_iota(jnp.int32, x.shape, 0)
+    half = LAT // 2
+    moved = jnp.where(slot < half, pltpu.roll(x, 1, 0), pltpu.roll(x, LAT - 1, 0))
+    return jnp.where(slot == LAT - 1, swap_halves(x), jnp.where(slot == 0, 0.0, moved))
+
+
+def filter_body(
+    band_ref, recv_ref, p_in, pt_in, gain_in, taps_ref, send_out, wide, out, p_ref, pt_ref, gain_ref, send_ref, sems
+):
     cuts = [pl.ds(4 * i, 4) for i in range(2)]
     tables = []
     for i, at in enumerate(cuts):
@@ -232,12 +252,31 @@
     shape = (LAT, 128)
     lane = lanes_of(shape)
     blank = jnp.zeros((32, 128), F32)
+    order = lax.broadcasted_iota(jnp.int32, (8, 128), 0) + band_ref[0] * 8
+    second = ((lanes_of((8, 128)) >> 5) & 1) == 1
+    highest = (order == 0) & second
+    turn_cosine = jnp.where(highest, -1.0, wave(order, 0, 1)) * (0.5 / math.pi)
+    turn_sine = jnp.where(second, -1.0, 1.0) * wave(order, 1, 1) * (0.5 / math.pi)
+    used = jnp.where(highest, 0.0, 1.0)
+    taps = [taps_ref[i : i + 1, 0:128] for i in range(9)]
     for m in range(8):
-        chunks = []
+        chunks, partners = [], []
         for h in range(2):
             low, high = (wide[pl.ds(rows * h + 8 * p + m, LAT, stride=16), :] for p in range(2))
             for s in range(4):
                 chunks.append(jnp.where(lane < 32, turn(low, -32 * s), turn(high, 32 - 32 * s)))
+                partners.append(jnp.where(lane < 32, turn(high, -32 * s), turn(low, 32 - 32 * s)))
+        mixed = []
+        for i in range(3):
+            west, here, east = taps[3 * i : 3 * i + 3]
+            along = here * (0.5 / math.pi) + (west + east) * turn_cosine[m : m + 1, :]
+            across = (east - west) * turn_sine[m : m + 1, :]
+            mixed.append([along * chunks[r] + across * partners[r] for r in range(8)])
+        above = [row_before(mixed[0][7])] + mixed[0][:7]
+        below = mixed[2][1:] + [row_after(mixed[2][0])]
+        local = [above[r] + mixed[1][r] + below[r] for r in range(8)]
+        if m == 0:
+            chunks = [chunk * used[0:1, :] for chunk in chunks]
         mirrored = [swap_halves(chunks[7 - r]) for r in range(4)]
         even = jnp.concatenate([chunks[r] + mirrored[r] for r in range(4)] + [blank], axis=0).astype(BF)
         odd = jnp.concatenate([chunks[r] - mirrored[r] for r in range(4)] + [blank], axis=0).astype(BF)
@@ -257,6 +296,7 @@
         near, far = halves_back[0] + halves_back[1], halves_back[0] - halves_back[1]
         back = [near[LAT * r : LAT * r + LAT, :] for r in range(4)]
         back = back + [swap_halves(far[LAT * r : LAT * r + LAT, :]) for r in (3, 2, 1, 0)]
+        back = [back[r] + local[r] for r in range(8)]
         for p in range(2):
             for h in range(2):
                 total = jnp.zeros(shape, F32)
@@ -271,38 +311,12 @@
     begin(send_ref, send_out, sems.at[5]).wait()
 
 
-def local_body(full_in, above_ref, below_ref, taps_ref, base_out, full_ref, base_ref, up, down, sems):
-    begin(full_in, full_ref, sems.at[0]).wait()
-    shape = (96, 128)
-    lane = lanes_of(shape)
-    for g in range(4):
-        at = slice(96 * g, 96 * g + 96)
-        left, right = full_ref[at, 0:128].astype(F32), full_ref[at, 128:256].astype(F32)
-        above, below = above_ref[...].astype(F32), below_ref[...].astype(F32)
-        up[at, 0:128] = jnp.where(lane < 32, turn(above, -32 * g), turn(left, 32))
-        up[at, 128:256] = jnp.where(lane < 32, turn(left, 32), turn(right, 32))
-        down[at, 0:128] = jnp.where(lane >= 96, turn(right, 96), turn(left, 96))
-        down[at, 128:256] = jnp.where(lane >= 96, turn(below, 96 - 32 * g), turn(right, 96))
-
-    def mixed(kap, b):
-        at = slice(32 * kap, 32 * kap + 32)
-        rows = (up[at, :], full_ref[at, :].astype(F32), down[at, :])
-        return sum(taps_ref[3 * i + b : 3 * i + b + 1, :] * rows[i] for i in range(3))
-
-    for kap in range(COLS):
-        west = mixed(kap - 1, 0) if kap > 0 else pltpu.roll(mixed(COLS - 1, 0), 1, 0)
-        east = mixed(kap + 1, 2) if kap < COLS - 1 else pltpu.roll(mixed(0, 2), LON - 1, 0)
-        at = slice(32 * kap, 32 * kap + 32)
-        base_ref[at, :] = (full_ref[at, :].astype(F32) + (west + mixed(kap, 1) + east)).astype(BF)
-    begin(base_ref, base_out, sems.at[1]).wait()
-
-
 def synthesis_body(recv_ref, base_in, send_out, inv_ref, base_ref, send_ref, out, summed_ref, sems):
     base = begin(base_in, base_ref, sems.at[0])
     shape = (LON, NLON)
     order, part = mode_of(lanes_of(shape))
     column = COLS * lax.broadcasted_iota(jnp.int32, shape, 0)
-    weight = jnp.where(order == 0, 1.0, 2.0)
+    weight = jnp.where((order == 0) | (order == NLON // 2), 1.0, 2.0)
     cosine, sine = wave(order, part, column) * weight, wave(order, part + 1, column) * weight
     shape = (16, NLON)
     order, _ = mode_of(lanes_of(shape))
@@ -367,52 +381,44 @@
     fhi, flo, taps = call(
         fourier_body,
         [(table, BF, VMEM), (table, BF, VMEM), ((16, 256), F32, VMEM)],
-        [(sector, SMEM), (conv_weight, VMEM)],
+        [(sector, SMEM), (conv_weight, HBM)],
+        [VMEM(conv_weight.shape, F32), pltpu.SemaphoreType.DMA],
         name="fourier_tables",
         flops=10_000_000,
     )
-    modes, full, first, last = call(
-        spectrum_body,
-        [(mode, BF, HBM), (circle, BF, HBM), ((96, 128), BF, HBM), ((96, 128), BF, HBM)],
-        [(band, SMEM), (pieces, VMEM), (fhi, VMEM), (flo, VMEM)],
-        [VMEM((LON * 16, 128), F32), VMEM(circle, BF), VMEM(mode, BF), VMEM((2, 96, 128), BF), pltpu.SemaphoreType.DMA((4,))],
-        name="spectrum",
-    )
-    modes = lax.all_to_all(modes, "lat", 0, 0, tiled=True, axis_index_groups=[SLOTS])
     polynomials = (8, NLAT, 128)
-    p, pt = call(
+    p, pt, gain = call(
         legendre_body,
-        [(polynomials, BF, HBM)] * 2,
-        [(band, SMEM)],
-        [VMEM((NLAT * 8, 128), F32), VMEM(polynomials, BF), VMEM(polynomials, BF), pltpu.SemaphoreType.DMA((4,))],
+        [(polynomials, BF, HBM), (polynomials, BF, HBM), ((NLAT, 128), F32, HBM)],
+        [(band, SMEM), (spectral_filter, HBM)],
+        [VMEM((NLAT * 8, 128), F32), VMEM(polynomials, BF), VMEM(polynomials, BF)]
+        + [VMEM((NLAT, 128), F32), VMEM((CHAN, NLAT), F32), VMEM((128, 256), F32), pltpu.SemaphoreType.DMA((6,))],
         name="legendre_tables",
         flops=10_000_000,
     )
-    gain = jnp.tile(jnp.pad(jnp.transpose(spectral_filter), ((0, 0), (0, 32 - CHAN))), (1, 4))
+    norm_gain = norm_gain.reshape(1, channels)
+    modes, full = call(
+        spectrum_body,
+        [(mode, BF, HBM), (circle, BF, HBM)],
+        [(pieces, VMEM), (fhi, VMEM), (flo, VMEM), (gain, HBM), (norm_gain, HBM)],
+        [VMEM((LON * 16, 128), F32), VMEM(circle, BF), VMEM(mode, BF), pltpu.SemaphoreType.DMA((2,))],
+        name="spectrum",
+    )
+    modes = lax.all_to_all(modes, "lat", 0, 0, tiled=True, axis_index_groups=[SLOTS])
     modes = call(
         filter_body,
         [(mode, BF, HBM)],
-        [(modes, VMEM), (p, HBM), (pt, HBM), (gain, HBM)],
+        [(band, SMEM), (modes, VMEM), (p, HBM), (pt, HBM), (gain, HBM), (taps, VMEM)],
         [VMEM((2 * LAT * 16, 128), F32)] * 2
         + [VMEM(polynomials, BF)] * 2
         + [VMEM((NLAT, 128), F32), VMEM(mode, BF), pltpu.SemaphoreType.DMA((6,))],
         name="filter",
     )
     modes = lax.all_to_all(modes, "lat", 0, 0, tiled=True, axis_index_groups=[SLOTS])
-    below = lax.ppermute(first, "lat", [(i + 1, i) for i in range(LAT - 1)])
-    above = lax.ppermute(last, "lat", [(i, i + 1) for i in range(LAT - 1)])
-    base = call(
-        local_body,
-        [(circle, BF, HBM)],
-        [(full, HBM), (above, VMEM), (below, VMEM), (taps, VMEM)],
-        [VMEM(circle, BF)] * 2 + [VMEM(circle, F32)] * 2 + [pltpu.SemaphoreType.DMA((2,))],
-        name="local_mix",
-        flops=5_000_000,
-    )
     pieces = call(
         synthesis_body,
         [(group, BF, HBM)],
-        [(modes, VMEM), (base, HBM)],
+        [(modes, VMEM), (full, HBM)],
         [VMEM(table, BF), VMEM(circle, BF), VMEM(group, BF), VMEM((LON * 16, 128), F32), VMEM(circle, F32)]
         + [pltpu.SemaphoreType.DMA((2,))],
         name="synthesis",
@@ -421,7 +427,7 @@
     result = call(
         mlp_body,
         [((points, channels), BF, VMEM)],
-        [(pieces, VMEM), (norm_gain.reshape(1, channels), VMEM), (weight_in, VMEM), (weight_out, VMEM)],
+        [(pieces, VMEM), (norm_gain, VMEM), (weight_in, VMEM), (weight_out, VMEM)],
         [VMEM((points, channels), F32)],
         name="mlp",
     )

time: 98.3 us -> 96.9 us (0.986)
  the two profiles are of different devices: /device:TPU:25 before, /device:TPU:1 now
where the time goes in v3:
time: 96.9 us; the launch traced here: 96.4 us
  blocking collectives  54.8 us (57%)
  starting transfers between devices  18.6 us (19%)
  Pallas kernels  14.1 us (15%)
  waiting for transfers between devices  7.5 us (8%)
  local copies, waits for them, and re-layouts  1.28 us (1%)
    all_to_all x2, blocking collectives, on_device(): lax.all_to_all(modes, 'lat', 0, 0, tiled=True, axis_index_groups=[SLOTS])  33.8 us
    all_to_all x1, blocking collectives, on_device(): pieces = lax.all_to_all(pieces, 'lon', 0, 0, tiled=True)  21 us
    all_to_all x1, starting transfers between devices, on_device(): pieces = lax.all_to_all(pieces, 'lon', 0, 0, tiled=True)  18.6 us
    pallas_call x7, Pallas kernels, call(): pl.pallas_call(body, out_shape=[HBM(shape, kind) if space is HBM else jax...  14.1 us
    all_to_all x1, waiting for transfers between devices, on_device(): pieces = lax.all_to_all(pieces, 'lon', 0, 0, tiled=True)  7.5 us
  transfers between devices with their start and end apart: 1, of which 1 were waited for; matrix products, arithmetic and copies ran while one was open for 1% of the time, Pallas kernels for 4%

profile of v3, /device:TPU:1, one launch (start us, length us, event | category | flops | bytes accessed | tf_op | source)
XLA Modules:
  0.0 96.4 jit_solution(10010442164834249121)
XLA Ops:
  0.0 1.8 %pack.1 = bf16[32,16,128]{2,1,0:T(8,128)(2,1)} custom-call(bf16[96,640]{1,0:T(8,128)(2,1)} %bitcast.8), custom_call_target="tpu_custom_call" | custom-call | bytes 1000000 | tf_op jit(solution)/shard_map/pack/pallas_call | solution.py:36
  1.8 18.6 %all-to-all-start = ((bf16[32,16,128]{2,1,0:T(8,128)(2,1)}), bf16[32,16,128]{2,1,0:T(8,128)(2,1)S(1)}, u32[]{:S(2)}, u32[]{:S(2)}) async-start(bf16[32,16,128]{2,1,0:T(8,128)(2,1)} %pack.1), calls=%async_computation | async-start | bytes 262144 | tf_op jit(solution)/shard_map/all_to_all | solution.py:377
  20.5 1.3 %reshape.18.unused_b.gain_ref = f32[1,640]{1,0:T(1,128)} reshape(f32[640]{0:T(1024)} %param.9) | data formatting | bytes 5120 | tf_op jit(solution)/shard_map/reshape | solution.py:399
  21.7 1.5 %fourier_tables.1 = (bf16[384,384]{1,0:T(8,128)(2,1)S(1)}, bf16[384,384]{1,0:T(8,128)(2,1)S(1)}, f32[16,256]{1,0:T(8,128)S(1)}) custom-call(s32[1]{0:T(128)} %bitcast.3.sector_ref, f32[9,640]{1,0:T(8,128)} %kernel_in.1), custom_call_target="tpu_custom_call" | custom-call | flops 10000000 | bytes 1000000 | tf_op jit(solution)/shard_map/fourier_tables/pallas_call | solution.py:36
  23.3 2.5 %legendre_tables.1 = (bf16[8,192,128]{2,1,0:T(8,128)(2,1)}, bf16[8,192,128]{2,1,0:T(8,128)(2,1)}, f32[192,128]{1,0:T(8,128)}) custom-call(s32[1]{0:T(128)} %bitcast.band_ref, f32[20,192]{1,0:T(8,128)} %gain_in.1), custom_call_target="tpu_custom_call" | custom-call | flops 10000000 | bytes 1000000 | tf_op jit(solution)/shard_map/legendre_tables/pallas_call | solution.py:36
  25.8 7.5 %all-to-all-done.recv_ref = bf16[32,16,128]{2,1,0:T(8,128)(2,1)S(1)} async-done(((bf16[32,16,128]{2,1,0:T(8,128)(2,1)}), bf16[32,16,128]{2,1,0:T(8,128)(2,1)S(1)}, u32[]{:S(2)}, u32[]{:S(2)}) %all-to-all-start) | async-done | bytes 131104 | tf_op jit(solution)/shard_map/all_to_all | solution.py:377
  33.3 0.0 copy-start.1
  33.3 1.3 %spectrum.1 = (bf16[24,16,256]{2,1,0:T(8,128)(2,1)}, bf16[384,256]{1,0:T(8,128)(2,1)}) custom-call(bf16[32,16,128]{2,1,0:T(8,128)(2,1)S(1)} %all-to-all-done.recv_ref, bf16[384,384]{1,0:T(8,128)(2,1)S(1)} %get-tuple-element.13.fhi_ref, bf16[384,384]{1,0:T(8,128)(2,1)S(1)} %get-tuple-element.14.flo_ref, f32[192,128]{1,0:T(8,128)} %get-tuple-element.15.unused_a.gain_in, ...), custom_call_target="tpu_custom_call" | custom-call | bytes 1000000 | tf_op jit(solution)/shard_map/spectrum/pallas_call | solution.py:36
  34.6 0.0 copy-start
  34.6 0.0 copy-start.2
  34.7 19.6 %all_to_all.20.recv_ref = bf16[24,16,256]{2,1,0:T(8,128)(2,1)S(1)} all-to-all(bf16[24,16,256]{2,1,0:T(8,128)(2,1)} %get-tuple-element.16), channel_id=1, replica_groups={{0,32,64,96,128,160,192,224,256,288,320,352,736,704,672,640,608,576,544..., dimensions={0} | all-to-all | bytes 393216 | tf_op jit(solution)/shard_map/all_to_all | solution.py:407
  54.2 3.0 %filter.1 = bf16[24,16,256]{2,1,0:T(8,128)(2,1)} custom-call(s32[1]{0:T(128)} %bitcast.band_ref, bf16[24,16,256]{2,1,0:T(8,128)(2,1)S(1)} %all_to_all.20.recv_ref, bf16[8,192,128]{2,1,0:T(8,128)(2,1)} %get-tuple-element.17.p_in, bf16[8,192,128]{2,1,0:T(8,128)(2,1)} %get-tuple-element.18.pt_in, f32[192,128]{1,0:T(8,128)} %get-tuple-element.15.unused_a.gain_in, ...), custom_call_target="tpu_custom_call" | custom-call | bytes 1000000 | tf_op jit(solution)/shard_map/filter/pallas_call | solution.py:36
  57.3 14.3 %all_to_all.21.recv_ref = bf16[24,16,256]{2,1,0:T(8,128)(2,1)S(1)} all-to-all(bf16[24,16,256]{2,1,0:T(8,128)(2,1)} %filter.1), channel_id=1, replica_groups={{0,32,64,96,128,160,192,224,256,288,320,352,736,704,672,640,608,576,544..., dimensions={0} | all-to-all | bytes 393216 | tf_op jit(solution)/shard_map/all_to_all | solution.py:417
  71.5 2.1 %synthesis.1 = bf16[32,16,128]{2,1,0:T(8,128)(2,1)} custom-call(bf16[24,16,256]{2,1,0:T(8,128)(2,1)S(1)} %all_to_all.21.recv_ref, bf16[384,256]{1,0:T(8,128)(2,1)} %get-tuple-element.20.base_in), custom_call_target="tpu_custom_call" | custom-call | bytes 1000000 | tf_op jit(solution)/shard_map/synthesis/pallas_call | solution.py:36
  73.7 21.0 %all_to_all.22.recv_ref = bf16[32,16,128]{2,1,0:T(8,128)(2,1)S(1)} all-to-all(bf16[32,16,128]{2,1,0:T(8,128)(2,1)} %synthesis.1), channel_id=1, replica_groups=mesh['lat'=24,'lon'=32] {'lon'}, dimensions={0} | all-to-all | bytes 262144 | tf_op jit(solution)/shard_map/all_to_all | solution.py:426
  94.6 0.0 copy-done.1
  94.6 0.0 copy-done
  94.7 0.0 copy-done.2
  94.7 1.7 %mlp.1 = bf16[96,640]{1,0:T(8,128)(2,1)} custom-call(bf16[32,16,128]{2,1,0:T(8,128)(2,1)S(1)} %all_to_all.22.recv_ref, f32[1,640]{1,0:T(1,128)S(1)} %copy-done.2, bf16[640,1280]{1,0:T(8,128)(2,1)S(1)} %copy-done, bf16[1280,640]{1,0:T(8,128)(2,1)S(1)} %copy-done.1), custom_call_target="tpu_custom_call" | custom-call | bytes 1000000 | tf_op jit(solution)/shard_map/mlp/pallas_call | solution.py:36
Async XLA Ops:
  1.8 31.5 %all-to-all-start = ((bf16[32,16,128]{2,1,0:T(8,128)(2,1)}), bf16[32,16,128]{2,1,0:T(8,128)(2,1)S(1)}, u32[]{:S(2)}, u32[]{:S(2)}) async-start(bf16[32,16,128]{2,1,0:T(8,128)(2,1)} %pack.1), calls=%async_computation | async-start | bytes 262144 | tf_op jit(solution)/shard_map/all_to_all | solution.py:377
  33.3 61.4 %copy-start.1 = (bf16[1280,640]{1,0:T(8,128)(2,1)S(1)}, bf16[1280,640]{1,0:T(8,128)(2,1)}, u32[]{:S(2)}) copy-start(bf16[1280,640]{1,0:T(8,128)(2,1)} %wout_ref.1) | copy-start | bytes 4915204
  34.6 60.0 %copy-start = (bf16[640,1280]{1,0:T(8,128)(2,1)S(1)}, bf16[640,1280]{1,0:T(8,128)(2,1)}, u32[]{:S(2)}) copy-start(bf16[640,1280]{1,0:T(8,128)(2,1)} %win_ref.1) | copy-start | bytes 4915204
  34.6 60.0 %copy-start.2 = (f32[1,640]{1,0:T(1,128)S(1)}, f32[1,640]{1,0:T(1,128)}, u32[]{:S(2)}) copy-start(f32[1,640]{1,0:T(1,128)} %reshape.18.unused_b.gain_ref) | copy-start | bytes 7684

commit v4 on v3

--- a/solution.py
+++ b/solution.py
@@ -133,10 +133,8 @@
     )
 
 
-def legendre_body(
-    band_ref, gain_in, p_out, pt_out, gain_out, table, p_ref, pt_ref, gain_ref, own_ref, square_ref, sems
-):
-    arriving = begin(gain_in, own_ref, sems.at[4])
+def legendre_body(band_ref, gain_in, p_ref, pt_ref, gain_ref, table, own_ref, square_ref, sem):
+    arriving = begin(gain_in, own_ref, sem)
     shape = (8, 128)
     lane = lanes_of(shape)
     order_i = lax.broadcasted_iota(jnp.int32, shape, 0) + band_ref[0] * 8
@@ -174,7 +172,6 @@
 
     blank = jnp.zeros(shape, F32)
     lax.fori_loop(0, NLAT // every, block, (blank, blank, start))
-    copies = []
     arriving.wait()
     square_ref[0:CHAN, 0:NLAT] = own_ref[...]
     for h in range(2):
@@ -182,7 +179,6 @@
         piece = jnp.where(lanes_of((128, 128)) < CHAN, piece, 0.0)
         height = 128 if h == 0 else NLAT - 128
         gain_ref[128 * h : 128 * h + height, :] = (piece + turn(piece, 32))[:height, :]
-    copies.append(begin(gain_ref, gain_out, sems.at[5]))
     weight = sine[0:1, :] * (math.pi / NLAT)
     blank = jnp.zeros((128 - NLAT // 2, 128), F32)
     for m in range(8):
@@ -191,15 +187,9 @@
             p_ref[m, 96 * parity : 96 * parity + 96, :] = (p * weight).astype(BF)
             turned = jnp.transpose(jnp.concatenate([p, blank], axis=0))
             pt_ref[m, 96 * parity : 96 * parity + 96, :] = turned[:96, :].astype(BF)
-        if m % 4 == 3:
-            at = pl.ds(m - 3, 4)
-            copies.append(begin(p_ref.at[at], p_out.at[at], sems.at[m // 4]))
-            copies.append(begin(pt_ref.at[at], pt_out.at[at], sems.at[2 + m // 4]))
-    for copy in copies:
-        copy.wait()
-
-
-def spectrum_body(recv_ref, fhi_ref, flo_ref, unused_a, unused_b, send_out, full_out, wide, full_ref, send_ref, sems):
+
+
+def spectrum_body(recv_ref, fhi_ref, flo_ref, unused_a, unused_b, send_out, full_ref, wide, send_ref, sem):
     wide[...] = recv_ref[...].astype(F32).reshape(LON * 16, 128)
     shape = (LON, 128)
     for e in range(2):
@@ -212,14 +202,11 @@
             for q in range(PAIRS):
                 kap = 2 * q + e
                 full_ref[32 * kap : 32 * kap + 32, 128 * h : 128 * h + 128] = total[q].astype(BF)
-    copies = [begin(full_ref, full_out, sems.at[1])]
     full = full_ref[...]
     spectrum = jnp.dot(fhi_ref[...], full, preferred_element_type=F32)
     spectrum = spectrum + jnp.dot(flo_ref[...], full, preferred_element_type=F32)
     send_ref[...] = spectrum.astype(BF).reshape(LAT, 16, 256)
-    copies.append(begin(send_ref, send_out, sems.at[0]))
-    for copy in copies:
-        copy.wait()
+    begin(send_ref, send_out, sem).wait()
 
 
 def row_after(x):
@@ -237,15 +224,8 @@
 
 
 def filter_body(
-    band_ref, recv_ref, p_in, pt_in, gain_in, taps_ref, send_out, wide, out, p_ref, pt_ref, gain_ref, send_ref, sems
+    band_ref, recv_ref, p_ref, pt_ref, gain_ref, taps_ref, send_out, wide, out, send_ref, sem
 ):
-    cuts = [pl.ds(4 * i, 4) for i in range(2)]
-    tables = []
-    for i, at in enumerate(cuts):
-        tables.append([begin(p_in.at[at], p_ref.at[at], sems.at[2 * i])])
-        if i == 0:
-            tables[0].append(begin(gain_in, gain_ref, sems.at[4]))
-        tables[i].append(begin(pt_in.at[at], pt_ref.at[at], sems.at[2 * i + 1]))
     rows = LAT * 16
     for h in range(2):
         wide[rows * h : rows * h + rows, :] = recv_ref[:, :, 128 * h : 128 * h + 128].astype(F32).reshape(rows, 128)
@@ -280,9 +260,6 @@
         mirrored = [swap_halves(chunks[7 - r]) for r in range(4)]
         even = jnp.concatenate([chunks[r] + mirrored[r] for r in range(4)] + [blank], axis=0).astype(BF)
         odd = jnp.concatenate([chunks[r] - mirrored[r] for r in range(4)] + [blank], axis=0).astype(BF)
-        if m % 4 == 0:
-            for copy in tables[m // 4]:
-                copy.wait()
         halves_back = []
         for parity in range(2):
             at = slice(96 * parity, 96 * parity + 96)
@@ -308,11 +285,10 @@
                 out[pl.ds(rows * h + 8 * p + m, LAT, stride=16), :] = total
     for h in range(2):
         send_ref[:, :, 128 * h : 128 * h + 128] = out[rows * h : rows * h + rows, :].astype(BF).reshape(LAT, 16, 128)
-    begin(send_ref, send_out, sems.at[5]).wait()
-
-
-def synthesis_body(recv_ref, base_in, send_out, inv_ref, base_ref, send_ref, out, summed_ref, sems):
-    base = begin(base_in, base_ref, sems.at[0])
+    begin(send_ref, send_out, sem).wait()
+
+
+def synthesis_body(recv_ref, base_ref, send_out, inv_ref, send_ref, out, summed_ref, sem):
     shape = (LON, NLON)
     order, part = mode_of(lanes_of(shape))
     column = COLS * lax.broadcasted_iota(jnp.int32, shape, 0)
@@ -326,7 +302,6 @@
         turned = cosine * step_cosine[kap : kap + 1, :] - sine * step_sine[kap : kap + 1, :]
         inv_ref[32 * kap : 32 * kap + 32, :] = turned.astype(BF)
     summed_ref[...] = jnp.dot(inv_ref[...], recv_ref[...].reshape(NLON, 256), preferred_element_type=F32)
-    base.wait()
     summed_ref[...] += base_ref[...].astype(F32)
     shape = (LON, 128)
     for e in range(2):
@@ -339,7 +314,7 @@
                     total = jnp.where(inside(shape, CHAN * q, CHAN), turn(rows, CHAN * q - 32 * s), total)
                 out[pl.ds(8 * e + 4 * h + s, LON, stride=16), :] = total
     send_ref[...] = out[...].astype(BF).reshape(LON, 16, 128)
-    begin(send_ref, send_out, sems.at[1]).wait()
+    begin(send_ref, send_out, sem).wait()
 
 
 def mlp_body(recv_ref, gain_ref, win_ref, wout_ref, out_ref, summed_ref):
@@ -389,38 +364,34 @@
     polynomials = (8, NLAT, 128)
     p, pt, gain = call(
         legendre_body,
-        [(polynomials, BF, HBM), (polynomials, BF, HBM), ((NLAT, 128), F32, HBM)],
+        [(polynomials, BF, VMEM), (polynomials, BF, VMEM), ((NLAT, 128), F32, VMEM)],
         [(band, SMEM), (spectral_filter, HBM)],
-        [VMEM((NLAT * 8, 128), F32), VMEM(polynomials, BF), VMEM(polynomials, BF)]
-        + [VMEM((NLAT, 128), F32), VMEM((CHAN, NLAT), F32), VMEM((128, 256), F32), pltpu.SemaphoreType.DMA((6,))],
+        [VMEM((NLAT * 8, 128), F32), VMEM((CHAN, NLAT), F32), VMEM((128, 256), F32), pltpu.SemaphoreType.DMA],
         name="legendre_tables",
         flops=10_000_000,
     )
     norm_gain = norm_gain.reshape(1, channels)
     modes, full = call(
         spectrum_body,
-        [(mode, BF, HBM), (circle, BF, HBM)],
-        [(pieces, VMEM), (fhi, VMEM), (flo, VMEM), (gain, HBM), (norm_gain, HBM)],
-        [VMEM((LON * 16, 128), F32), VMEM(circle, BF), VMEM(mode, BF), pltpu.SemaphoreType.DMA((2,))],
+        [(mode, BF, HBM), (circle, BF, VMEM)],
+        [(pieces, VMEM), (fhi, VMEM), (flo, VMEM), (gain, VMEM), (norm_gain, HBM)],
+        [VMEM((LON * 16, 128), F32), VMEM(mode, BF), pltpu.SemaphoreType.DMA],
         name="spectrum",
     )
     modes = lax.all_to_all(modes, "lat", 0, 0, tiled=True, axis_index_groups=[SLOTS])
     modes = call(
         filter_body,
         [(mode, BF, HBM)],
-        [(band, SMEM), (modes, VMEM), (p, HBM), (pt, HBM), (gain, HBM), (taps, VMEM)],
-        [VMEM((2 * LAT * 16, 128), F32)] * 2
-        + [VMEM(polynomials, BF)] * 2
-        + [VMEM((NLAT, 128), F32), VMEM(mode, BF), pltpu.SemaphoreType.DMA((6,))],
+        [(band, SMEM), (modes, VMEM), (p, VMEM), (pt, VMEM), (gain, VMEM), (taps, VMEM)],
+        [VMEM((2 * LAT * 16, 128), F32)] * 2 + [VMEM(mode, BF), pltpu.SemaphoreType.DMA],
         name="filter",
     )
     modes = lax.all_to_all(modes, "lat", 0, 0, tiled=True, axis_index_groups=[SLOTS])
     pieces = call(
         synthesis_body,
         [(group, BF, HBM)],
-        [(modes, VMEM), (full, HBM)],
-        [VMEM(table, BF), VMEM(circle, BF), VMEM(group, BF), VMEM((LON * 16, 128), F32), VMEM(circle, F32)]
-        + [pltpu.SemaphoreType.DMA((2,))],
+        [(modes, VMEM), (full, VMEM)],
+        [VMEM(table, BF), VMEM(group, BF), VMEM((LON * 16, 128), F32), VMEM(circle, F32), pltpu.SemaphoreType.DMA],
         name="synthesis",
     )
     pieces = lax.all_to_all(pieces, "lon", 0, 0, tiled=True)

time: 96.9 us -> 94.9 us (0.979)
  Pallas kernels: 14.1 us -> 11.3 us
    pallas_call x7, Pallas kernels: 14.1 us -> 11.3 us  [call(): pl.pallas_call(body, out_shape=[HBM(shape, kind) if space is HBM else jax...]
  transfers between devices with their start and end apart: 1 -> 1, of which waited for: 1 -> 1; matrix products, arithmetic and copies ran while one was open for 1% -> 1% of each run, Pallas kernels for 4% -> 3%
where the time goes in v4:
time: 94.9 us; the launch traced here: 94.4 us
  blocking collectives  54.8 us (58%)
  starting transfers between devices  18.6 us (20%)
  Pallas kernels  11.3 us (12%)
  waiting for transfers between devices  8.28 us (9%)
  local copies, waits for them, and re-layouts  1.29 us (1%)
    all_to_all x2, blocking collectives, on_device(): lax.all_to_all(modes, 'lat', 0, 0, tiled=True, axis_index_groups=[SLOTS])  33.8 us
    all_to_all x1, blocking collectives, on_device(): pieces = lax.all_to_all(pieces, 'lon', 0, 0, tiled=True)  21 us
    all_to_all x1, starting transfers between devices, on_device(): pieces = lax.all_to_all(pieces, 'lon', 0, 0, tiled=True)  18.6 us
    pallas_call x7, Pallas kernels, call(): pl.pallas_call(body, out_shape=[HBM(shape, kind) if space is HBM else jax...  11.3 us
    all_to_all x1, waiting for transfers between devices, on_device(): pieces = lax.all_to_all(pieces, 'lon', 0, 0, tiled=True)  8.28 us
  transfers between devices with their start and end apart: 1, of which 1 were waited for; matrix products, arithmetic and copies ran while one was open for 1% of the time, Pallas kernels for 3%

profile of v4, /device:TPU:1, one launch (start us, length us, event | category | flops | bytes accessed | tf_op | source)
XLA Modules:
  0.0 94.4 jit_solution(8027846674612363188)
XLA Ops:
  0.0 1.8 %pack.1 = bf16[32,16,128]{2,1,0:T(8,128)(2,1)} custom-call(bf16[96,640]{1,0:T(8,128)(2,1)} %bitcast.8), custom_call_target="tpu_custom_call" | custom-call | bytes 1000000 | tf_op jit(solution)/shard_map/pack/pallas_call | solution.py:36
  1.8 18.6 %all-to-all-start = ((bf16[32,16,128]{2,1,0:T(8,128)(2,1)}), bf16[32,16,128]{2,1,0:T(8,128)(2,1)S(1)}, u32[]{:S(2)}, u32[]{:S(2)}) async-start(bf16[32,16,128]{2,1,0:T(8,128)(2,1)} %pack.1), calls=%async_computation | async-start | bytes 262144 | tf_op jit(solution)/shard_map/all_to_all | solution.py:352
  20.5 1.3 %reshape.18.unused_b.gain_ref = f32[1,640]{1,0:T(1,128)} reshape(f32[640]{0:T(1024)} %param.9) | data formatting | bytes 5120 | tf_op jit(solution)/shard_map/reshape | solution.py:373
  21.7 1.5 %fourier_tables.1 = (bf16[384,384]{1,0:T(8,128)(2,1)S(1)}, bf16[384,384]{1,0:T(8,128)(2,1)S(1)}, f32[16,256]{1,0:T(8,128)S(1)}) custom-call(s32[1]{0:T(128)} %bitcast.3.sector_ref, f32[9,640]{1,0:T(8,128)} %kernel_in.1), custom_call_target="tpu_custom_call" | custom-call | flops 10000000 | bytes 1000000 | tf_op jit(solution)/shard_map/fourier_tables/pallas_call | solution.py:36
  23.3 1.7 %legendre_tables.1 = (bf16[8,192,128]{2,1,0:T(8,128)(2,1)S(1)}, bf16[8,192,128]{2,1,0:T(8,128)(2,1)S(1)}, f32[192,128]{1,0:T(8,128)S(1)}) custom-call(s32[1]{0:T(128)} %bitcast.band_ref, f32[20,192]{1,0:T(8,128)} %gain_in.1), custom_call_target="tpu_custom_call" | custom-call | flops 10000000 | bytes 1000000 | tf_op jit(solution)/shard_map/legendre_tables/pallas_call | solution.py:36
  25.0 8.3 %all-to-all-done.recv_ref = bf16[32,16,128]{2,1,0:T(8,128)(2,1)S(1)} async-done(((bf16[32,16,128]{2,1,0:T(8,128)(2,1)}), bf16[32,16,128]{2,1,0:T(8,128)(2,1)S(1)}, u32[]{:S(2)}, u32[]{:S(2)}) %all-to-all-start) | async-done | bytes 131104 | tf_op jit(solution)/shard_map/all_to_all | solution.py:352
  33.3 0.0 copy-start.1
  33.3 1.3 %spectrum.1 = (bf16[24,16,256]{2,1,0:T(8,128)(2,1)}, bf16[384,256]{1,0:T(8,128)(2,1)S(1)}) custom-call(bf16[32,16,128]{2,1,0:T(8,128)(2,1)S(1)} %all-to-all-done.recv_ref, bf16[384,384]{1,0:T(8,128)(2,1)S(1)} %get-tuple-element.13.fhi_ref, bf16[384,384]{1,0:T(8,128)(2,1)S(1)} %get-tuple-element.14.flo_ref, ...), custom_call_target="tpu_custom_call" | custom-call | bytes 1000000 | tf_op jit(solution)/shard_map/spectrum/pallas_call | solution.py:36
  34.6 0.0 copy-start
  34.6 0.0 copy-start.2
  34.6 19.6 %all_to_all.20.recv_ref = bf16[24,16,256]{2,1,0:T(8,128)(2,1)S(1)} all-to-all(bf16[24,16,256]{2,1,0:T(8,128)(2,1)} %get-tuple-element.16), channel_id=1, replica_groups={{0,32,64,96,128,160,192,224,256,288,320,352,736,704,672,640,608,576,544..., dimensions={0} | all-to-all | bytes 393216 | tf_op jit(solution)/shard_map/all_to_all | solution.py:381
  54.2 1.8 %filter.1 = bf16[24,16,256]{2,1,0:T(8,128)(2,1)} custom-call(s32[1]{0:T(128)} %bitcast.band_ref, bf16[24,16,256]{2,1,0:T(8,128)(2,1)S(1)} %all_to_all.20.recv_ref, bf16[8,192,128]{2,1,0:T(8,128)(2,1)S(1)} %get-tuple-element.17.p_ref, bf16[8,192,128]{2,1,0:T(8,128)(2,1)S(1)} %get-tuple-element.18.pt_ref, f32[192,128]{1,0:T(8,128)S(1)} %get-tuple-element.15.unused_a.gain_ref, ...), custom_call_target="tpu_custom_call" | custom-call | bytes 1000000 | tf_op jit(solution)/shard_map/filter/pallas_call | solution.py:36
  56.0 14.2 %all_to_all.21.recv_ref = bf16[24,16,256]{2,1,0:T(8,128)(2,1)S(1)} all-to-all(bf16[24,16,256]{2,1,0:T(8,128)(2,1)} %filter.1), channel_id=1, replica_groups={{0,32,64,96,128,160,192,224,256,288,320,352,736,704,672,640,608,576,544..., dimensions={0} | all-to-all | bytes 393216 | tf_op jit(solution)/shard_map/all_to_all | solution.py:389
  70.3 1.4 %synthesis.1 = bf16[32,16,128]{2,1,0:T(8,128)(2,1)} custom-call(bf16[24,16,256]{2,1,0:T(8,128)(2,1)S(1)} %all_to_all.21.recv_ref, bf16[384,256]{1,0:T(8,128)(2,1)S(1)} %get-tuple-element.20.base_ref), custom_call_target="tpu_custom_call" | custom-call | bytes 1000000 | tf_op jit(solution)/shard_map/synthesis/pallas_call | solution.py:36
  71.7 21.0 %all_to_all.22.recv_ref = bf16[32,16,128]{2,1,0:T(8,128)(2,1)S(1)} all-to-all(bf16[32,16,128]{2,1,0:T(8,128)(2,1)} %synthesis.1), channel_id=1, replica_groups=mesh['lat'=24,'lon'=32] {'lon'}, dimensions={0} | all-to-all | bytes 262144 | tf_op jit(solution)/shard_map/all_to_all | solution.py:397
  92.7 0.0 copy-done.1
  92.7 0.0 copy-done
  92.7 0.0 copy-done.2
  92.7 1.7 %mlp.1 = bf16[96,640]{1,0:T(8,128)(2,1)} custom-call(bf16[32,16,128]{2,1,0:T(8,128)(2,1)S(1)} %all_to_all.22.recv_ref, f32[1,640]{1,0:T(1,128)S(1)} %copy-done.2, bf16[640,1280]{1,0:T(8,128)(2,1)S(1)} %copy-done, bf16[1280,640]{1,0:T(8,128)(2,1)S(1)} %copy-done.1), custom_call_target="tpu_custom_call" | custom-call | bytes 1000000 | tf_op jit(solution)/shard_map/mlp/pallas_call | solution.py:36
Async XLA Ops:
  1.8 31.5 %all-to-all-start = ((bf16[32,16,128]{2,1,0:T(8,128)(2,1)}), bf16[32,16,128]{2,1,0:T(8,128)(2,1)S(1)}, u32[]{:S(2)}, u32[]{:S(2)}) async-start(bf16[32,16,128]{2,1,0:T(8,128)(2,1)} %pack.1), calls=%async_computation | async-start | bytes 262144 | tf_op jit(solution)/shard_map/all_to_all | solution.py:352
  33.3 59.4 %copy-start.1 = (bf16[1280,640]{1,0:T(8,128)(2,1)S(1)}, bf16[1280,640]{1,0:T(8,128)(2,1)}, u32[]{:S(2)}) copy-start(bf16[1280,640]{1,0:T(8,128)(2,1)} %wout_ref.1) | copy-start | bytes 4915204
  34.6 58.1 %copy-start = (bf16[640,1280]{1,0:T(8,128)(2,1)S(1)}, bf16[640,1280]{1,0:T(8,128)(2,1)}, u32[]{:S(2)}) copy-start(bf16[640,1280]{1,0:T(8,128)(2,1)} %win_ref.1) | copy-start | bytes 4915204
  34.6 58.1 %copy-start.2 = (f32[1,640]{1,0:T(1,128)S(1)}, f32[1,640]{1,0:T(1,128)}, u32[]{:S(2)}) copy-start(f32[1,640]{1,0:T(1,128)} %reshape.18.unused_b.gain_ref) | copy-start | bytes 7684

commit v5 on v4

--- a/solution.py
+++ b/solution.py
@@ -109,7 +109,7 @@
     return high, (x - high.astype(F32)).astype(BF)
 
 
-def fourier_body(sector_ref, kernel_in, fhi_ref, flo_ref, taps_ref, kernel_ref, sem):
+def fourier_body(sector_ref, kernel_in, fhi_ref, flo_ref, taps_ref, inv_ref, kernel_ref, sem):
     arriving = begin(kernel_in, kernel_ref, sem)
     shape = (16, NLON)
     lane = lanes_of(shape)
@@ -123,6 +123,18 @@
         return unused
 
     lax.fori_loop(0, NLON // 16, block, 0)
+    shape = (LON, NLON)
+    order, part = mode_of(lanes_of(shape))
+    column = COLS * lax.broadcasted_iota(jnp.int32, shape, 0)
+    weight = jnp.where((order == 0) | (order == NLON // 2), 1.0, 2.0)
+    cosine, sine = wave(order, part, column) * weight, wave(order, part + 1, column) * weight
+    shape = (16, NLON)
+    order, _ = mode_of(lanes_of(shape))
+    column = lax.broadcasted_iota(jnp.int32, shape, 0)
+    step_cosine, step_sine = wave(order, 0, column), wave(order, 1, column)
+    for kap in range(COLS):
+        turned = cosine * step_cosine[kap : kap + 1, :] - sine * step_sine[kap : kap + 1, :]
+        inv_ref[32 * kap : 32 * kap + 32, :] = turned.astype(BF)
     arriving.wait()
     wide = (kernel_ref.shape[1], 256)
     own = lanes_of(wide) & 31
@@ -288,19 +300,7 @@
     begin(send_ref, send_out, sem).wait()
 
 
-def synthesis_body(recv_ref, base_ref, send_out, inv_ref, send_ref, out, summed_ref, sem):
-    shape = (LON, NLON)
-    order, part = mode_of(lanes_of(shape))
-    column = COLS * lax.broadcasted_iota(jnp.int32, shape, 0)
-    weight = jnp.where((order == 0) | (order == NLON // 2), 1.0, 2.0)
-    cosine, sine = wave(order, part, column) * weight, wave(order, part + 1, column) * weight
-    shape = (16, NLON)
-    order, _ = mode_of(lanes_of(shape))
-    column = lax.broadcasted_iota(jnp.int32, shape, 0)
-    step_cosine, step_sine = wave(order, 0, column), wave(order, 1, column)
-    for kap in range(COLS):
-        turned = cosine * step_cosine[kap : kap + 1, :] - sine * step_sine[kap : kap + 1, :]
-        inv_ref[32 * kap : 32 * kap + 32, :] = turned.astype(BF)
+def synthesis_body(recv_ref, base_ref, inv_ref, send_out, send_ref, out, summed_ref, sem):
     summed_ref[...] = jnp.dot(inv_ref[...], recv_ref[...].reshape(NLON, 256), preferred_element_type=F32)
     summed_ref[...] += base_ref[...].astype(F32)
     shape = (LON, 128)
@@ -317,7 +317,7 @@
     begin(send_ref, send_out, sem).wait()
 
 
-def mlp_body(recv_ref, gain_ref, win_ref, wout_ref, out_ref, summed_ref):
+def mlp_body(recv_ref, gain_ref, win_ref, wout_ref, result_out, summed_ref, out_ref, sems):
     shape = (16, 128)
     lane = lanes_of(shape)
     for tile in range(5):
@@ -333,8 +333,15 @@
     normed = (summed * lax.rsqrt(mean + EPS) * gain_ref[...]).astype(BF)
     hidden = jnp.dot(normed, win_ref[...], preferred_element_type=F32)
     hidden = (0.5 * hidden * (1.0 + lax.erf(hidden * math.sqrt(0.5)))).astype(BF)
-    result = summed + jnp.dot(hidden, wout_ref[...], preferred_element_type=F32)
-    out_ref[...] = result.astype(BF)
+    copies = []
+    for i, (start, width) in enumerate(((0, 384), (384, 256))):
+        at = slice(start, start + width)
+        result = summed_ref[:, at] + jnp.dot(hidden, wout_ref[:, at], preferred_element_type=F32)
+        out_ref[:, at] = result.astype(BF)
+        at = pl.ds(start, width)
+        copies.append(begin(out_ref.at[:, at], result_out.at[:, at], sems.at[i]))
+    for copy in copies:
+        copy.wait()
 
 
 def on_device(latent_field, spectral_filter, conv_weight, norm_gain, weight_in, weight_out):
@@ -353,9 +360,9 @@
 
     sector = lax.axis_index("lon").astype(jnp.int32).reshape(1)
     band = lax.axis_index("lat").astype(jnp.int32).reshape(1)
-    fhi, flo, taps = call(
+    fhi, flo, taps, inverse = call(
         fourier_body,
-        [(table, BF, VMEM), (table, BF, VMEM), ((16, 256), F32, VMEM)],
+        [(table, BF, VMEM), (table, BF, VMEM), ((16, 256), F32, VMEM), (table, BF, VMEM)],
         [(sector, SMEM), (conv_weight, HBM)],
         [VMEM(conv_weight.shape, F32), pltpu.SemaphoreType.DMA],
         name="fourier_tables",
@@ -390,16 +397,16 @@
     pieces = call(
         synthesis_body,
         [(group, BF, HBM)],
-        [(modes, VMEM), (full, VMEM)],
-        [VMEM(table, BF), VMEM(group, BF), VMEM((LON * 16, 128), F32), VMEM(circle, F32), pltpu.SemaphoreType.DMA],
+        [(modes, VMEM), (full, VMEM), (inverse, VMEM)],
+        [VMEM(group, BF), VMEM((LON * 16, 128), F32), VMEM(circle, F32), pltpu.SemaphoreType.DMA],
         name="synthesis",
     )
     pieces = lax.all_to_all(pieces, "lon", 0, 0, tiled=True)
     result = call(
         mlp_body,
-        [((points, channels), BF, VMEM)],
+        [((points, channels), BF, HBM)],
         [(pieces, VMEM), (norm_gain, VMEM), (weight_in, VMEM), (weight_out, VMEM)],
-        [VMEM((points, channels), F32)],
+        [VMEM((points, channels), F32), VMEM((points, channels), BF), pltpu.SemaphoreType.DMA((2,))],
         name="mlp",
     )
     return jnp.transpose(result.reshape(COLS, ROWS, channels), (2, 1, 0))

time: 94.9 us -> 94.8 us (level)
  transfers between devices with their start and end apart: 1 -> 1, of which waited for: 1 -> 1; matrix products, arithmetic and copies ran while one was open for 1% -> 1% of each run, Pallas kernels for 3% -> 4%
where the time goes in v5:
time: 94.8 us; the launch traced here: 94.3 us
  blocking collectives  54.8 us (58%)
  starting transfers between devices  18.6 us (20%)
  Pallas kernels  11.5 us (12%)
  waiting for transfers between devices  8.05 us (8%)
  local copies, waits for them, and re-layouts  1.29 us (1%)
    all_to_all x2, blocking collectives, on_device(): lax.all_to_all(modes, 'lat', 0, 0, tiled=True, axis_index_groups=[SLOTS])  33.8 us
    all_to_all x1, blocking collectives, on_device(): pieces = lax.all_to_all(pieces, 'lon', 0, 0, tiled=True)  21 us
    all_to_all x1, starting transfers between devices, on_device(): pieces = lax.all_to_all(pieces, 'lon', 0, 0, tiled=True)  18.6 us
    pallas_call x7, Pallas kernels, call(): pl.pallas_call(body, out_shape=[HBM(shape, kind) if space is HBM else jax...  11.5 us
    all_to_all x1, waiting for transfers between devices, on_device(): pieces = lax.all_to_all(pieces, 'lon', 0, 0, tiled=True)  8.05 us
  transfers between devices with their start and end apart: 1, of which 1 were waited for; matrix products, arithmetic and copies ran while one was open for 1% of the time, Pallas kernels for 4%

profile of v5, /device:TPU:1, one launch (start us, length us, event | category | flops | bytes accessed | tf_op | source)
XLA Modules:
  0.0 94.3 jit_solution(9022713924739043998)
XLA Ops:
  0.0 1.8 %pack.1 = bf16[32,16,128]{2,1,0:T(8,128)(2,1)} custom-call(bf16[96,640]{1,0:T(8,128)(2,1)} %bitcast.8), custom_call_target="tpu_custom_call" | custom-call | bytes 1000000 | tf_op jit(solution)/shard_map/pack/pallas_call | solution.py:36
  1.8 18.6 %all-to-all-start = ((bf16[32,16,128]{2,1,0:T(8,128)(2,1)}), bf16[32,16,128]{2,1,0:T(8,128)(2,1)S(1)}, u32[]{:S(2)}, u32[]{:S(2)}) async-start(bf16[32,16,128]{2,1,0:T(8,128)(2,1)} %pack.1), calls=%async_computation | async-start | bytes 262144 | tf_op jit(solution)/shard_map/all_to_all | solution.py:359
  20.5 1.3 %reshape.18.unused_b.gain_ref = f32[1,640]{1,0:T(1,128)} reshape(f32[640]{0:T(1024)} %param.9) | data formatting | bytes 5120 | tf_op jit(solution)/shard_map/reshape | solution.py:380
  21.7 1.7 %legendre_tables.1 = (bf16[8,192,128]{2,1,0:T(8,128)(2,1)S(1)}, bf16[8,192,128]{2,1,0:T(8,128)(2,1)S(1)}, f32[192,128]{1,0:T(8,128)S(1)}) custom-call(s32[1]{0:T(128)} %bitcast.band_ref, f32[20,192]{1,0:T(8,128)} %gain_in.1), custom_call_target="tpu_custom_call" | custom-call | flops 10000000 | bytes 1000000 | tf_op jit(solution)/shard_map/legendre_tables/pallas_call | solution.py:36
  23.5 1.8 %fourier_tables.1 = (bf16[384,384]{1,0:T(8,128)(2,1)S(1)}, bf16[384,384]{1,0:T(8,128)(2,1)S(1)}, f32[16,256]{1,0:T(8,128)S(1)}, bf16[384,384]{1,0:T(8,128)(2,1)S(1)}) custom-call(s32[1]{0:T(128)} %bitcast.3.sector_ref, f32[9,640]{1,0:T(8,128)} %kernel_in.1), custom_call_target="tpu_custom_call" | custom-call | flops 10000000 | bytes 1000000 | tf_op jit(solution)/shard_map/fourier_tables/pallas_call | solution.py:36
  25.2 8.1 %all-to-all-done.recv_ref = bf16[32,16,128]{2,1,0:T(8,128)(2,1)S(1)} async-done(((bf16[32,16,128]{2,1,0:T(8,128)(2,1)}), bf16[32,16,128]{2,1,0:T(8,128)(2,1)S(1)}, u32[]{:S(2)}, u32[]{:S(2)}) %all-to-all-start) | async-done | bytes 131104 | tf_op jit(solution)/shard_map/all_to_all | solution.py:359
  33.3 0.0 copy-start.1
  33.3 1.3 %spectrum.1 = (bf16[24,16,256]{2,1,0:T(8,128)(2,1)}, bf16[384,256]{1,0:T(8,128)(2,1)S(1)}) custom-call(bf16[32,16,128]{2,1,0:T(8,128)(2,1)S(1)} %all-to-all-done.recv_ref, bf16[384,384]{1,0:T(8,128)(2,1)S(1)} %get-tuple-element.14.fhi_ref, bf16[384,384]{1,0:T(8,128)(2,1)S(1)} %get-tuple-element.15.flo_ref, ...), custom_call_target="tpu_custom_call" | custom-call | bytes 1000000 | tf_op jit(solution)/shard_map/spectrum/pallas_call | solution.py:36
  34.6 0.0 copy-start
  34.6 0.0 copy-start.2
  34.6 19.6 %all_to_all.20.recv_ref = bf16[24,16,256]{2,1,0:T(8,128)(2,1)S(1)} all-to-all(bf16[24,16,256]{2,1,0:T(8,128)(2,1)} %get-tuple-element.17), channel_id=1, replica_groups={{0,32,64,96,128,160,192,224,256,288,320,352,736,704,672,640,608,576,544..., dimensions={0} | all-to-all | bytes 393216 | tf_op jit(solution)/shard_map/all_to_all | solution.py:388
  54.2 1.8 %filter.1 = bf16[24,16,256]{2,1,0:T(8,128)(2,1)} custom-call(s32[1]{0:T(128)} %bitcast.band_ref, bf16[24,16,256]{2,1,0:T(8,128)(2,1)S(1)} %all_to_all.20.recv_ref, bf16[8,192,128]{2,1,0:T(8,128)(2,1)S(1)} %get-tuple-element.18.p_ref, bf16[8,192,128]{2,1,0:T(8,128)(2,1)S(1)} %get-tuple-element.19.pt_ref, f32[192,128]{1,0:T(8,128)S(1)} %get-tuple-element.16.unused_a.gain_ref, ...), custom_call_target="tpu_custom_call" | custom-call | bytes 1000000 | tf_op jit(solution)/shard_map/filter/pallas_call | solution.py:36
  56.0 14.2 %all_to_all.21.recv_ref = bf16[24,16,256]{2,1,0:T(8,128)(2,1)S(1)} all-to-all(bf16[24,16,256]{2,1,0:T(8,128)(2,1)} %filter.1), channel_id=1, replica_groups={{0,32,64,96,128,160,192,224,256,288,320,352,736,704,672,640,608,576,544..., dimensions={0} | all-to-all | bytes 393216 | tf_op jit(solution)/shard_map/all_to_all | solution.py:396
  70.3 1.3 %synthesis.1 = bf16[32,16,128]{2,1,0:T(8,128)(2,1)} custom-call(bf16[24,16,256]{2,1,0:T(8,128)(2,1)S(1)} %all_to_all.21.recv_ref, bf16[384,256]{1,0:T(8,128)(2,1)S(1)} %get-tuple-element.21.base_ref, bf16[384,384]{1,0:T(8,128)(2,1)S(1)} %get-tuple-element.22.inv_ref), custom_call_target="tpu_custom_call" | custom-call | bytes 1000000 | tf_op jit(solution)/shard_map/synthesis/pallas_call | solution.py:36
  71.6 21.0 %all_to_all.22.recv_ref = bf16[32,16,128]{2,1,0:T(8,128)(2,1)S(1)} all-to-all(bf16[32,16,128]{2,1,0:T(8,128)(2,1)} %synthesis.1), channel_id=1, replica_groups=mesh['lat'=24,'lon'=32] {'lon'}, dimensions={0} | all-to-all | bytes 262144 | tf_op jit(solution)/shard_map/all_to_all | solution.py:404
  92.6 0.0 copy-done.1
  92.6 0.0 copy-done
  92.6 0.0 copy-done.2
  92.6 1.7 %mlp.1 = bf16[96,640]{1,0:T(8,128)(2,1)} custom-call(bf16[32,16,128]{2,1,0:T(8,128)(2,1)S(1)} %all_to_all.22.recv_ref, f32[1,640]{1,0:T(1,128)S(1)} %copy-done.2, bf16[640,1280]{1,0:T(8,128)(2,1)S(1)} %copy-done, bf16[1280,640]{1,0:T(8,128)(2,1)S(1)} %copy-done.1), custom_call_target="tpu_custom_call" | custom-call | bytes 1000000 | tf_op jit(solution)/shard_map/mlp/pallas_call | solution.py:36
Async XLA Ops:
  1.8 31.5 %all-to-all-start = ((bf16[32,16,128]{2,1,0:T(8,128)(2,1)}), bf16[32,16,128]{2,1,0:T(8,128)(2,1)S(1)}, u32[]{:S(2)}, u32[]{:S(2)}) async-start(bf16[32,16,128]{2,1,0:T(8,128)(2,1)} %pack.1), calls=%async_computation | async-start | bytes 262144 | tf_op jit(solution)/shard_map/all_to_all | solution.py:359
  33.3 59.3 %copy-start.1 = (bf16[1280,640]{1,0:T(8,128)(2,1)S(1)}, bf16[1280,640]{1,0:T(8,128)(2,1)}, u32[]{:S(2)}) copy-start(bf16[1280,640]{1,0:T(8,128)(2,1)} %wout_ref.1) | copy-start | bytes 4915204
  34.6 58.0 %copy-start = (bf16[640,1280]{1,0:T(8,128)(2,1)S(1)}, bf16[640,1280]{1,0:T(8,128)(2,1)}, u32[]{:S(2)}) copy-start(bf16[640,1280]{1,0:T(8,128)(2,1)} %win_ref.1) | copy-start | bytes 4915204
  34.6 58.0 %copy-start.2 = (f32[1,640]{1,0:T(1,128)S(1)}, f32[1,640]{1,0:T(1,128)}, u32[]{:S(2)}) copy-start(f32[1,640]{1,0:T(1,128)} %reshape.18.unused_b.gain_ref) | copy-start | bytes 7684
